TPU v7x, 32 devices: a whole 2x2x4 slice. The times are simulated.
32 devices in a mesh: dp: 4 (over y, x), fsdp: 8 (over z, core).
Axes of the slice: x: 2, y: 2, z: 4, core: 2. Of those that a mesh axis runs over, the one named last changes fastest.
Arguments:
- inputs: bfloat16 [65536, 1280], P(('dp', 'fsdp')), may hold values from -6 to 6
- lengths: int32 [32, 8], P(('dp', 'fsdp')), may hold values from 1 to 1024, 2048 in all within a row
- keep_mask: int32 [65536], P(('dp', 'fsdp')), may hold values 0 or 1
- cotangent: bfloat16 [65536, 1280], P(('dp', 'fsdp')), may hold values from -6 to 6
- ln1_gain: bfloat16 [1280], P(('dp', 'fsdp')), may hold values from 0.099609375 to 1.8984375
- ln1_bias: bfloat16 [1280], P(('dp', 'fsdp')), may hold values from -3 to 3
- up_weight: bfloat16 [1280, 640], P(('dp', 'fsdp')), may hold values from -0.15625 to 0.15625
- up_bias: bfloat16 [640], P(('dp', 'fsdp')), may hold values from -3 to 3
- ln2_gain: bfloat16 [640], P(('dp', 'fsdp')), may hold values from 0.099609375 to 1.8984375
- ln2_bias: bfloat16 [640], P(('dp', 'fsdp')), may hold values from -3 to 3
- conv_weight: bfloat16 [5, 640, 640], P(None, ('dp', 'fsdp')), may hold values from -0.109375 to 0.109375
- conv_bias: bfloat16 [640], P(('dp', 'fsdp')), may hold values from -3 to 3
- ln3_gain: bfloat16 [640], P(('dp', 'fsdp')), may hold values from 0.099609375 to 1.8984375
- ln3_bias: bfloat16 [640], P(('dp', 'fsdp')), may hold values from -3 to 3
- down_weight: bfloat16 [640, 1280], P(None, ('dp', 'fsdp')), may hold values from -0.3125 to 0.3125
- down_bias: bfloat16 [1280], P(('dp', 'fsdp')), may hold values from -3 to 3
Outputs:
- output: bfloat16 [65536, 1280], P(('dp', 'fsdp'))
- input_grad: float32 [65536, 1280], P(('dp', 'fsdp'))
- up_weight_grad: float32 [1280, 640], P(('dp', 'fsdp'))
- conv_weight_grad: float32 [5, 640, 640], P(None, ('dp', 'fsdp'))
- down_weight_grad: float32 [640, 1280], P(None, ('dp', 'fsdp'))
- ln1_gain_grad: float32 [1280], P(('dp', 'fsdp'))
- ln1_bias_grad: float32 [1280], P(('dp', 'fsdp'))
- up_bias_grad: float32 [640], P(('dp', 'fsdp'))
- ln2_gain_grad: float32 [640], P(('dp', 'fsdp'))
- ln2_bias_grad: float32 [640], P(('dp', 'fsdp'))
- conv_bias_grad: float32 [640], P(('dp', 'fsdp'))
- ln3_gain_grad: float32 [640], P(('dp', 'fsdp'))
- ln3_bias_grad: float32 [640], P(('dp', 'fsdp'))
- down_bias_grad: float32 [1280], P(('dp', 'fsdp'))
Inputs may be any that keep to these rules, and one draw needn't show every extreme that they name: `lengths`: each row sums to 2048; the largest entry of every row is 1024.
All inputs are finite; a program needn't handle non-finite values. No bound on the sum of `keep_mask` on one device may be relied on, other than what follows from the above.
Results may differ from a plain program's by a relative error of at most 0.0068.
Values may be sent and summed in bfloat16 or wider, within the bound.
No kernel may reach another device: no remote copies, remote signals or barrier semaphores. Data moves between devices by JAX's collectives and lax.ppermute only.
A program may use at most 192 MiB of HBM per device.

v0:
```python
import jax
import jax.numpy as jnp
from jax import lax
from jax.sharding import PartitionSpec as P

KERNEL = 5
DILATION = 8


def norm_act(field, gain, shift):
    center = field - jnp.mean(field, axis=-1, keepdims=True)
    spread = jnp.mean(center * center, axis=-1, keepdims=True)
    return jax.nn.gelu(center * lax.rsqrt(spread + 1e-05) * gain + shift)


def tap_masks(lengths_row, count):
    seq_ends = jnp.cumsum(lengths_row)
    position = jnp.arange(count, dtype=jnp.int32)
    segment = jnp.sum((position[:, None] >= seq_ends[None, :]).astype(jnp.int32), axis=1)
    masks = []
    for tap in range(KERNEL):
        source = position + (tap - KERNEL // 2) * DILATION
        inside = (source >= 0) & (source < count)
        matched = segment[jnp.clip(source, 0, count - 1)] == segment
        masks.append(jnp.where(inside & matched, 1.0, 0.0))
    return jnp.stack(masks).astype(jnp.float32)


def first_dims(left, right):
    return lax.dot_general(
        left, right, (((0,), (0,)), ((), ())), preferred_element_type=jnp.float32
    )


def last_dims(left, right):
    return lax.dot_general(
        left, right, (((1,), (1,)), ((), ())), preferred_element_type=jnp.float32
    )


def body(
    inputs,
    lengths,
    keep_mask,
    cotangent,
    ln1_gain,
    ln1_bias,
    up_weight,
    up_bias,
    ln2_gain,
    ln2_bias,
    conv_weight,
    conv_bias,
    ln3_gain,
    ln3_bias,
    down_weight,
    down_bias,
):
    gathered = (
        lax.all_gather(up_weight, ("dp", "fsdp"), axis=0, tiled=True),
        lax.all_gather(conv_weight, ("dp", "fsdp"), axis=1, tiled=True),
        lax.all_gather(down_weight, ("dp", "fsdp"), axis=1, tiled=True),
        lax.all_gather(ln1_gain, ("dp", "fsdp"), axis=0, tiled=True),
        lax.all_gather(ln1_bias, ("dp", "fsdp"), axis=0, tiled=True),
        lax.all_gather(up_bias, ("dp", "fsdp"), axis=0, tiled=True),
        lax.all_gather(ln2_gain, ("dp", "fsdp"), axis=0, tiled=True),
        lax.all_gather(ln2_bias, ("dp", "fsdp"), axis=0, tiled=True),
        lax.all_gather(conv_bias, ("dp", "fsdp"), axis=0, tiled=True),
        lax.all_gather(ln3_gain, ("dp", "fsdp"), axis=0, tiled=True),
        lax.all_gather(ln3_bias, ("dp", "fsdp"), axis=0, tiled=True),
        lax.all_gather(down_bias, ("dp", "fsdp"), axis=0, tiled=True),
    )
    up_full, conv_full, down_full = (gathered[0], gathered[1], gathered[2])
    (
        gain_one,
        bias_one,
        up_shift,
        gain_two,
        bias_two,
        conv_shift,
        gain_three,
        bias_three,
        down_shift,
    ) = [item.astype(jnp.float32) for item in gathered[3:]]
    count = inputs.shape[0]
    reach = KERNEL // 2 * DILATION
    masks = tap_masks(lengths[0], count)
    keep_col = keep_mask.astype(jnp.float32)[:, None]
    x_float = inputs.astype(jnp.float32)
    act_first, back_one = jax.vjp(norm_act, x_float, gain_one, bias_one)
    act_one = act_first.astype(jnp.bfloat16)
    up_out = jnp.dot(act_one, up_full, preferred_element_type=jnp.float32) + up_shift

    def masked_act(field, gain, shift):
        return norm_act(field, gain, shift) * keep_col

    act_second, back_two = jax.vjp(masked_act, up_out, gain_two, bias_two)
    middle = act_second.astype(jnp.bfloat16)
    padded = jnp.pad(middle, ((reach, reach), (0, 0)))
    taps = [
        padded[tap * DILATION : tap * DILATION + count] * masks[tap][:, None].astype(jnp.bfloat16)
        for tap in range(KERNEL)
    ]
    conv_sum = jnp.dot(taps[0], conv_full[0], preferred_element_type=jnp.float32)
    for tap in range(1, KERNEL):
        conv_sum = conv_sum + jnp.dot(taps[tap], conv_full[tap], preferred_element_type=jnp.float32)
    conv_out = conv_sum + conv_shift
    act_third, back_three = jax.vjp(norm_act, conv_out, gain_three, bias_three)
    act_top = act_third.astype(jnp.bfloat16)
    output = (
        x_float + jnp.dot(act_top, down_full, preferred_element_type=jnp.float32) + down_shift
    ).astype(jnp.bfloat16)
    up_back, conv_back, down_back = (
        lax.all_gather(up_weight, ("dp", "fsdp"), axis=0, tiled=True),
        lax.all_gather(conv_weight, ("dp", "fsdp"), axis=1, tiled=True),
        lax.all_gather(down_weight, ("dp", "fsdp"), axis=1, tiled=True),
    )
    grad_out = cotangent.astype(jnp.float32)
    down_shift_grad = jnp.sum(grad_out, axis=0)
    down_grad = first_dims(act_top, cotangent)
    top_grad = last_dims(cotangent, down_back)
    conv_grad, gain_three_grad, bias_three_grad = back_three(top_grad)
    conv_shift_grad = jnp.sum(conv_grad, axis=0)
    conv_low = conv_grad.astype(jnp.bfloat16)
    conv_grad_weight = jnp.stack([first_dims(tap_in, conv_low) for tap_in in taps])
    padded_grad = jnp.zeros((count + 2 * reach, conv_low.shape[1]), jnp.float32)
    for tap in range(KERNEL):
        term = last_dims(conv_low, conv_back[tap]) * masks[tap][:, None]
        padded_grad = padded_grad.at[tap * DILATION : tap * DILATION + count].add(term)
    middle_grad = padded_grad[reach : reach + count]
    up_grad, gain_two_grad, bias_two_grad = back_two(middle_grad)
    up_shift_grad = jnp.sum(up_grad, axis=0)
    up_low = up_grad.astype(jnp.bfloat16)
    up_grad_weight = first_dims(act_one, up_low)
    act_grad = last_dims(up_low, up_back)
    skip_grad, gain_one_grad, bias_one_grad = back_one(act_grad)
    input_grad = grad_out + skip_grad
    owned = (
        lax.psum_scatter(up_grad_weight, ("dp", "fsdp"), scatter_dimension=0, tiled=True),
        lax.psum_scatter(conv_grad_weight, ("dp", "fsdp"), scatter_dimension=1, tiled=True),
        lax.psum_scatter(down_grad, ("dp", "fsdp"), scatter_dimension=1, tiled=True),
        lax.psum_scatter(gain_one_grad, ("dp", "fsdp"), scatter_dimension=0, tiled=True),
        lax.psum_scatter(bias_one_grad, ("dp", "fsdp"), scatter_dimension=0, tiled=True),
        lax.psum_scatter(up_shift_grad, ("dp", "fsdp"), scatter_dimension=0, tiled=True),
        lax.psum_scatter(gain_two_grad, ("dp", "fsdp"), scatter_dimension=0, tiled=True),
        lax.psum_scatter(bias_two_grad, ("dp", "fsdp"), scatter_dimension=0, tiled=True),
        lax.psum_scatter(conv_shift_grad, ("dp", "fsdp"), scatter_dimension=0, tiled=True),
        lax.psum_scatter(gain_three_grad, ("dp", "fsdp"), scatter_dimension=0, tiled=True),
        lax.psum_scatter(bias_three_grad, ("dp", "fsdp"), scatter_dimension=0, tiled=True),
        lax.psum_scatter(down_shift_grad, ("dp", "fsdp"), scatter_dimension=0, tiled=True),
    )
    return (output, input_grad) + tuple(owned)


def solution(mesh):
    in_specs = (
        P(("dp", "fsdp"), None),
        P(("dp", "fsdp"), None),
        P(("dp", "fsdp")),
        P(("dp", "fsdp"), None),
        P(("dp", "fsdp")),
        P(("dp", "fsdp")),
        P(("dp", "fsdp"), None),
        P(("dp", "fsdp")),
        P(("dp", "fsdp")),
        P(("dp", "fsdp")),
        P(None, ("dp", "fsdp"), None),
        P(("dp", "fsdp")),
        P(("dp", "fsdp")),
        P(("dp", "fsdp")),
        P(None, ("dp", "fsdp")),
        P(("dp", "fsdp")),
    )
    out_specs = (
        P(("dp", "fsdp"), None),
        P(("dp", "fsdp"), None),
        P(("dp", "fsdp"), None),
        P(None, ("dp", "fsdp"), None),
        P(None, ("dp", "fsdp")),
        P(("dp", "fsdp")),
        P(("dp", "fsdp")),
        P(("dp", "fsdp")),
        P(("dp", "fsdp")),
        P(("dp", "fsdp")),
        P(("dp", "fsdp")),
        P(("dp", "fsdp")),
        P(("dp", "fsdp")),
        P(("dp", "fsdp")),
    )
    return jax.shard_map(body, mesh=mesh, in_specs=in_specs, out_specs=out_specs, check_vma=False)
```

profile of v0, /device:TPU:0, one launch (start us, length us, event | category | flops | bytes accessed | tf_op | source)
XLA Modules:
  0.0 699.6 jit_solution(5362989921846986815)
XLA Ops:
  7.2 0.7 all-gather.4.cloned.1.call-update
  8.0 1.6 copy.57
  9.6 0.7 all-gather.8.cloned.1.call-update
  10.5 0.8 dynamic-update-slice.22
  11.4 0.8 dynamic-update-slice.20
  12.2 0.8 dynamic-update-slice.17
  13.0 0.8 dynamic-update-slice.18
  13.9 0.8 dynamic-update-slice.19
  14.7 0.8 dynamic-update-slice.21
  15.5 0.8 dynamic-update-slice.16
  16.4 0.8 dynamic-update-slice.23
  17.2 0.8 dynamic-update-slice.15
  18.1 42.5 %all-reduce.24 = (bf16[1280]{0:T(1024)(128)(2,1)S(1)}, bf16[640]{0:T(1024)(128)(2,1)S(1)}, bf16[640]{0:T(1024)(128)(2,1)S(1)}, bf16[1280]{0:T(1024)(128)(2,1)S(1...) all-reduce(bf16[1280]{0:T(1024)(128)(2,1)S(1)} %dynamic-update-slic, ...), channel_id=1, replica_groups=mesh['dp'=4,'fsdp'=8] {'dp','fsdp'}, use_global_device_ids=true, to_apply=%add.10 | all-reduce | flops 7680 | bytes 30720
  60.6 0.8 reduce-window.8
  61.6 0.9 convert_element_type.106
  62.4 3.5 convert_reduce_fusion
  66.0 1.5 fusion.19
  67.5 11.8 %gather_fusion = s32[2048]{0:T(1024)S(1)} fusion(s32[2048]{0:T(1024)S(1)} %convert_reduce_fusion.2, s32[2048]{0:T(1024)S(1)} %broadcast_clamp_fusion.4), kind=kCustom, calls=%fused_computation | custom fusion | bytes 24576 | tf_op jit(solution)/shard_map/gather | solution.py:24
  79.3 11.8 %gather_fusion.2 = s32[2048]{0:T(1024)S(1)} fusion(s32[2048]{0:T(1024)S(1)} %convert_reduce_fusion.2, s32[2048]{0:T(1024)S(1)} %get-tuple-element.142), kind=kCustom, calls=%fused_computation.2 | custom fusion | bytes 24576 | tf_op jit(solution)/shard_map/gather | solution.py:24
  91.1 11.8 %gather_fusion.1 = s32[2048]{0:T(1024)S(1)} fusion(s32[2048]{0:T(1024)S(1)} %convert_reduce_fusion.2, s32[2048]{0:T(1024)S(1)} %get-tuple-element.143), kind=kCustom, calls=%fused_computation.1 | custom fusion | bytes 24576 | tf_op jit(solution)/shard_map/gather | solution.py:24
  102.9 11.8 %gather_fusion.4 = s32[2048]{0:T(1024)S(1)} fusion(s32[2048]{0:T(1024)S(1)} %convert_reduce_fusion.2, s32[2048]{0:T(1024)S(1)} %get-tuple-element.140), kind=kCustom, calls=%fused_computation.4 | custom fusion | bytes 24576 | tf_op jit(solution)/shard_map/gather | solution.py:24
  114.7 11.8 %gather_fusion.3 = s32[2048]{0:T(1024)S(1)} fusion(s32[2048]{0:T(1024)S(1)} %convert_reduce_fusion.2, s32[2048]{0:T(1024)S(1)} %get-tuple-element.141), kind=kCustom, calls=%fused_computation.3 | custom fusion | bytes 24576 | tf_op jit(solution)/shard_map/gather | solution.py:24
  126.5 8.3 %fusion.12 = bf16[2048,1280]{1,0:T(8,128)(2,1)} fusion(bf16[2048,1280]{1,0:T(8,128)(2,1)} %param.26, f32[1280]{0:T(1024)S(1)} %convert_element_type.101, f32[1280]{0:T(1024)S(1)} %convert_element_type.100, f32[2048]{0:T(1024)S(1)} %fusion.91, f32[2048]{0:T(1024)S(1)} %broadcast_multiply_fusion.2), kind=kLoop, calls=%fused_computation.25 | loop fusion | flops 36700160 | bytes 10512384 | tf_op jit(solution)/shard_map/convert_element_type | solution.py:91
  134.9 6.9 add_reduce_fusion.2
  141.8 1.0 multiply_reduce_fusion.5
  142.8 1.3 copy-done.1
  144.1 3.2 multiply_convert_fusion.1
  147.3 19.9 %fusion.120 = (bf16[1,640,640]{2,0,1:T(2,128)(2,1)S(1)}, bf16[1,640,640]{2,0,1:T(2,128)(2,1)S(1)}, bf16[1,640,640]{2,0,1:T(2,128)(2,1)S(1)}, bf16[1,640,640]{2,0,1:T(2,128)(2,1)S(1)}, bf16[1,640,640]{2,0,1:T(2,128)(2,1)S(1)}) fusion(bf16[5,640,640]{2,0,1:T(8,128)(2,1)} %all-gather.6.cloned.1.call-done), kind=kLoop, calls=%fused_computation.197 | loop fusion | bytes 8192000 | tf_op jit(solution)/shard_map/slice | solution.py:106
  167.2 2.6 fusion.45
  169.9 2.6 fusion.47
  172.5 4.4 fusion.43
  176.9 4.3 fusion.40
  181.2 6.4 fusion.121
  187.5 2.3 copy-done.2
  189.9 0.8 multiply_reduce_fusion.4
  190.7 8.1 %all-gather.8.cloned.1.call-done = bf16[640,1280]{0,1:T(8,128)(2,1)} async-done(((bf16[640,40]{0,1:T(8,128)(2,1)}), bf16[640,1280]{0,1:T(8,128)(2,1)}) %all-gather.8.cloned.1.call-update) | async-done | bytes 1638416 | tf_op jit(solution)/shard_map/all_gather | solution.py:62
  198.8 12.0 %multiply_reduce_fusion = (f32[640]{0:T(1024)S(1)}, f32[2048]{0:T(1024)S(1)}, f32[640]{0:T(1024)S(1)}, f32[2048,640]{1,0:T(8,128)S(1)}) fusion(f32[2048,640]{1,0:T(8,128)} %copy-done.2, f32[2048]{0:T(1024)S(1)} %fusion.93, f32[2048]{0:T(1024)S(1)} %broadcast_multiply_fusion, f32[640]{0:T(1024)S(1)} %convert_element_type.115, ...), kind=kOutput, calls=%fused_computation.61 | convolution fusion | flops 3393451008 | bytes 17401856 | tf_op jit(solution)/shard_map/dot_general | solution.py:36
  210.9 2.4 fusion.108
  213.8 1.2 copy-done.7
  215.0 3.7 bitcast_dynamic-update-slice_fusion.4
  218.7 3.6 bitcast_dynamic-update-slice_fusion.3
  222.4 3.6 bitcast_dynamic-update-slice_fusion.2
  226.0 3.6 bitcast_dynamic-update-slice_fusion.1
  229.6 3.6 bitcast_dynamic-update-slice_fusion
  233.8 11.0 %fusion.104 = f32[640,1280]{0,1:T(8,128)} fusion(bf16[2048,1280]{1,0:T(8,128)(2,1)} %param.29, f32[2048,640]{1,0:T(8,128)} %copy-done.2, f32[640]{0:T(1024)S(1)} %convert_element_type.116, f32[640]{0:T(1024)S(1)} %convert_element_type.115, f32[2048]{0:T(1024)S(1)} %fusion.93, f32[2048]{0:T(1024)S(1)} %broadcast_multiply_fusion), kind=kOutput, calls=%fused_computation.188 | convolution fusion | flops 3372482560 | bytes 13784064 | tf_op jit(solution)/shard_map/dot_general | solution.py:30
  244.8 4.1 convolution_multiply_fusion
  249.3 1.1 copy-done.15
  250.4 2.8 add_dynamic-update-slice_fusion
  253.2 2.8 fusion.37
  256.1 2.8 fusion.36
  258.9 3.0 fusion.35
  261.9 6.7 multiply_reduce_fusion.1
  268.7 2.6 fusion.106
  271.3 2.3 copy-done.4
  273.7 6.2 fusion.102
  279.9 15.7 %fusion.105 = (f32[1280]{0:T(1024)S(1)}, f32[2048]{0:T(1024)S(1)}, f32[2048,1280]{1,0:T(8,128)S(1)}) fusion(f32[1280]{0:T(1024)S(1)} %convert_element_type.100, f32[2048]{0:T(1024)S(1)} %broadcast_multiply_fusion.2, bf16[2048,1280]{1,0:T(8,128)(2,1)} %param.26, f32[1280]{0:T(1024)S(1)} %convert_element_type.101, f32[2048]{0:T(1024)S(1)} %fusion.91, ...), kind=kOutput, calls=%fused_computation.189 | convolution fusion | flops 3431461632 | bytes 22658048 | tf_op jit(solution)/shard_map/dot_general | solution.py:36
  295.8 5.6 fusion.15
  301.9 6.9 convert_reduce_fusion.1
  308.8 39.8 %all-reduce.23 = (f32[1280]{0:T(1024)S(1)}, f32[1280]{0:T(1024)S(1)}, f32[640]{0:T(1024)S(1)}, f32[640]{0:T(1024)S(1)}, f32[640]{0:T(1024)S(1)}, /*index=5*/f32[...) all-reduce(f32[1280]{0:T(1024)S(1)} %get-tuple-element.74, ...), channel_id=5, replica_groups=mesh['dp'=4,'fsdp'=8] {'dp','fsdp'}, use_global_device_ids=true, to_apply=%region_18.19.clone | all-reduce | flops 7680 | bytes 61440
  353.8 10.8 %fusion.22 = bf16[2048,1280]{1,0:T(8,128)(2,1)} fusion(bf16[2048,1280]{1,0:T(8,128)(2,1)} %param.26, bf16[640,1280]{0,1:T(8,128)(2,1)} %all-gather.8.cloned.1.call-done, f32[1280]{0:T(1024)S(1)} %convert_element_type.118, f32[2048,640]{1,0:T(8,128)} %copy-done.2, f32[640]{0:T(1024)S(1)} %convert_element_type.116, f32[640]{0:T(1024)S(1)} %convert_element_type.115, ...), kind=kOutput, calls=%fused_computation.35 | convolution fusion | flops 3382968320 | bytes 17393664 | tf_op jit(solution)/shard_map/dot_general | solution.py:111
  364.6 45.1 %all-reduce.27.cloned.1.call-done = f32[5,640,640]{2,1,0:T(8,128)} async-done(((f32[5,640,640]{2,1,0:T(8,128)}), f32[5,640,640]{2,1,0:T(8,128)}) %all-reduce.27.cloned.1.call-update) | async-done | bytes 8192016
  409.8 1.7 constant_dynamic-slice_fusion
  411.5 141.5 %reduce-scatter.12.cloned.1.call-done = f32[640,40]{0,1:T(8,128)} async-done(((f32[640,1280]{0,1:T(8,128)}), f32[640,40]{0,1:T(8,128)}) %reduce-scatter.12.cloned.1.call-update) | async-done | bytes 102416
  553.0 139.5 %reduce-scatter.10.cloned.1.call-done = f32[40,640]{1,0:T(8,128)} async-done(((f32[1280,640]{1,0:T(8,128)}), f32[40,640]{1,0:T(8,128)}) %reduce-scatter.10.cloned.1.call-update) | async-done | bytes 102416
  (117 shorter events, 7.7 us)
Async XLA Ops:
  7.2 127.7 %all-gather.4.cloned.1.call-start = ((), (), s32[]{:S(2)}) async-start(), calls=%async_computation.2 | async-start | bytes 1689600 | tf_op jit(solution)/shard_map/all_gather | solution.py:60
  7.9 139.4 %all-gather.6.cloned.1.call-start = ((), (), s32[]{:S(2)}) async-start(), calls=%async_computation.3 | async-start | bytes 6758400 | tf_op jit(solution)/shard_map/all_gather | solution.py:61
  9.6 189.2 %all-gather.8.cloned.1.call-start = ((), (), s32[]{:S(2)}) async-start(), calls=%async_computation.4 | async-start | bytes 1689600 | tf_op jit(solution)/shard_map/all_gather | solution.py:62
  10.3 399.4 %all-reduce.27.cloned.1.call-start = ((), (), s32[]{:S(2)}) async-start(), calls=%async_computation.5 | async-start | bytes 16384000
  61.5 4.5 copy-start
  67.5 23.6 %copy-start.17 = (f32[2048]{0:T(1024)}, f32[2048]{0:T(1024)S(1)}, u32[]{:S(2)}) copy-start(f32[2048]{0:T(1024)S(1)} %fusion.19) | copy-start | bytes 24580
  141.8 2.3 copy-start.1
  147.3 33.9 %copy-start.6 = (bf16[2048,640]{1,0:T(8,128)(2,1)}, bf16[2048,640]{1,0:T(8,128)(2,1)S(1)}, u32[]{:S(2)}) copy-start(bf16[2048,640]{1,0:T(8,128)(2,1)S(1)} %multiply_convert_fusion.1) | copy-start | bytes 7864324
  167.2 2.7 copy-start.14
  167.2 2.7 copy-start.10
  167.2 5.3 copy-start.16
  167.2 9.7 %copy-start.12 = (bf16[1,640,640]{2,0,1:T(2,128)(2,1)}, bf16[1,640,640]{2,0,1:T(2,128)(2,1)S(1)}, u32[]{:S(2)}) copy-start(bf16[1,640,640]{2,0,1:T(2,128)(2,1)S(1)} %get-tuple-element.120) | copy-start | bytes 2457604
  167.2 13.9 %copy-start.8 = (bf16[1,640,640]{2,0,1:T(2,128)(2,1)}, bf16[1,640,640]{2,0,1:T(2,128)(2,1)S(1)}, u32[]{:S(2)}) copy-start(bf16[1,640,640]{2,0,1:T(2,128)(2,1)S(1)} %get-tuple-element.118) | copy-start | bytes 2457604
  187.5 2.3 copy-start.2
  198.8 12.1 %copy-start.3 = (f32[2048,640]{1,0:T(8,128)S(1)}, f32[2048,640]{1,0:T(8,128)}, u32[]{:S(2)}) copy-start(f32[2048,640]{1,0:T(8,128)} %copy-done.2) | copy-start | bytes 15728644
  213.3 1.7 copy-start.7
  233.3 319.7 %reduce-scatter.12.cloned.1.call-start = ((), (), s32[]{:S(2)}) async-start(), calls=%async_computation.7 | async-start | bytes 3379200
  244.8 447.7 %reduce-scatter.10.cloned.1.call-start = ((), (), s32[]{:S(2)}) async-start(), calls=%async_computation.6 | async-start | bytes 3379200
  249.0 1.4 copy-start.15
  250.4 2.8 copy-start.13
  253.2 2.8 copy-start.11
  256.1 2.8 copy-start.9
  256.1 5.8 slice-start.2
  258.9 3.0 slice-start.3
  261.9 11.7 %slice-start.4 = ((s8[5242880]{0:T(1024)(128)(4,1)}), s8[4194304]{0:T(1024)(128)(4,1)S(1)}, s32[]{:S(2)}) async-start(s8[5242880]{0:T(1024)(128)(4,1)} %bitcast.63), calls=%async_computation.12 | async-start | bytes 8388608
  268.7 5.0 slice-start.5
  271.3 2.4 copy-start.4
  273.7 22.1 %slice-start = ((s8[5242880]{0:T(1024)(128)(4,1)}), s8[1048576]{0:T(1024)(128)(4,1)S(1)}, s32[]{:S(2)}) async-start(s8[5242880]{0:T(1024)(128)(4,1)} %bitcast.59), calls=%async_computation.8 | async-start | bytes 2097152
  279.9 15.8 %copy-start.18 = (f32[2048]{0:T(1024)S(1)}, f32[2048]{0:T(1024)}, u32[]{:S(2)}) copy-start(f32[2048]{0:T(1024)} %copy-done.17) | copy-start | bytes 24580
  279.9 15.8 %slice-start.1 = ((s8[5242880]{0:T(1024)(128)(4,1)}), s8[4194304]{0:T(1024)(128)(4,1)S(1)}, s32[]{:S(2)}) async-start(s8[5242880]{0:T(1024)(128)(4,1)} %bitcast.59), calls=%async_computation.9 | async-start | bytes 8388608
  295.7 6.2 slice-start.6
  295.8 5.7 copy-start.5
  295.8 6.1 slice-start.7
Sparse Core Ops, SparseCore 0:
  10.8 58.2 all-gather.3
  72.6 69.6 all-gather.5
  145.1 53.7 all-gather.7
  233.4 176.2 all-reduce.26
  412.5 140.5 reduce-scatter.11
  555.8 136.6 reduce-scatter.9
where the time goes:
time: 709 us; the launch traced here: 700 us
  waiting for transfers between devices  336 us (47%)
  matrix products  117 us (17%)
  local copies, waits for them, and re-layouts  104 us (15%)
  blocking collectives  82.3 us (12%)
  other arithmetic  45.5 us (6%)
  between operations  15.2 us (2%)
    unnamed x9, waiting for transfers between devices  328 us
    unnamed x2, blocking collectives  82.3 us
    gather x5, local copies, waits for them, and re-layouts, tap_masks(): matched = segment[jnp.clip(source, 0, count - 1)] == segment  58.9 us
    dot_general x7, matrix products, last_dims(): lax.dot_general(left, right, (((1,), (1,)), ((), ())), preferred_element_...  43.3 us
    dot_general x7, matrix products, first_dims(): lax.dot_general(left, right, (((0,), (0,)), ((), ())), preferred_element_...  35.5 us
    unnamed x83, local copies, waits for them, and re-layouts  24.4 us
    slice x1, local copies, waits for them, and re-layouts, body(): conv_full[tap]  19.9 us
    dot_general x4, matrix products, body(): jnp.dot(taps[tap], conv_full[tap], preferred_element_type=jnp.float32)  15.9 us
  transfers between devices with their start and end apart: 6, of which 4 were waited for; matrix products, arithmetic and copies ran while one was open for 32% of the time, Pallas kernels for 0%

commit v1 on v0

v1 whole, which is shorter than its diff:
```python
import functools

import jax
import jax.numpy as jnp
from jax import lax
from jax.sharding import Mesh
from jax.sharding import PartitionSpec as P

KERNEL = 5
DILATION = 8
ALL = ("dp", "chip", "core")


def norm_act(field, gain, shift):
    center = field - jnp.mean(field, axis=-1, keepdims=True)
    spread = jnp.mean(center * center, axis=-1, keepdims=True)
    return jax.nn.gelu(center * lax.rsqrt(spread + 1e-05) * gain + shift)


def segments(ends, position):
    return jnp.sum((position[:, None] >= ends[None, :]).astype(jnp.int32), axis=1)


def tap_masks(lengths_row, count):
    ends = jnp.cumsum(lengths_row)
    position = jnp.arange(count, dtype=jnp.int32)
    own = segments(ends, position)
    masks = []
    for tap in range(KERNEL):
        source = position + (tap - KERNEL // 2) * DILATION
        inside = (source >= 0) & (source < count)
        masks.append(jnp.where(inside & (segments(ends, source) == own), 1.0, 0.0))
    return jnp.stack(masks).astype(jnp.float32)


def xor_order(items, me):
    bit = 1
    while bit < len(items):
        there = (me & bit) != 0
        items = [jnp.where(there, items[k ^ bit], items[k]) for k in range(len(items))]
        bit *= 2
    return items


def first_dims(left, right):
    return lax.dot_general(
        left, right, (((0,), (0,)), ((), ())), preferred_element_type=jnp.float32
    )


def last_dims(left, right):
    return lax.dot_general(
        left, right, (((1,), (1,)), ((), ())), preferred_element_type=jnp.float32
    )


def swap(array, axis, size, mask):
    return lax.ppermute(array, axis, [(k, k ^ mask) for k in range(size)])


def gather_axis(array, axis, size, place):
    held = [array] + [swap(array, axis, size, mask) for mask in range(1, size)]
    return jnp.stack(xor_order(held, lax.axis_index(axis)), place)


def scatter_axis(array, axis, size, place):
    blocks = [lax.index_in_dim(array, k, place, False) for k in range(size)]
    blocks = xor_order(blocks, lax.axis_index(axis))
    total = blocks[0]
    for mask in range(1, size):
        arrived = swap(blocks[mask].astype(jnp.bfloat16), axis, size, mask)
        total = total + arrived.astype(jnp.float32)
    return total


def gather_all(block, axes):
    out = gather_axis(block, axes[1][0], axes[1][1], 0)
    out = gather_axis(out, axes[0][0], axes[0][1], 0)
    out = gather_axis(out, axes[2][0], axes[2][1], 2)
    return out.reshape((-1,) + block.shape)


def scatter_all(blocks, axes):
    sizes = tuple(size for _, size in axes)
    out = blocks.reshape(sizes + blocks.shape[1:])
    out = scatter_axis(out, axes[2][0], axes[2][1], 2)
    out = scatter_axis(out, axes[0][0], axes[0][1], 0)
    return scatter_axis(out, axes[1][0], axes[1][1], 0)


def body(
    axes,
    inputs,
    lengths,
    keep_mask,
    cotangent,
    ln1_gain,
    ln1_bias,
    up_weight,
    up_bias,
    ln2_gain,
    ln2_bias,
    conv_weight,
    conv_bias,
    ln3_gain,
    ln3_bias,
    down_weight,
    down_bias,
):
    vectors = (ln1_gain, ln1_bias, up_bias, ln2_gain, ln2_bias, conv_bias, ln3_gain, ln3_bias, down_bias)
    widths = [item.shape[0] for item in vectors]
    devices = axes[0][1] * axes[1][1] * axes[2][1]
    taps_in, inner = conv_weight.shape[1], conv_weight.shape[2]
    small = gather_all(jnp.concatenate(vectors)[None, :], axes)[:, 0]
    full_vectors, at = [], 0
    for width in widths:
        full_vectors.append(small[:, at : at + width].reshape(-1).astype(jnp.float32))
        at += width
    (
        gain_one,
        bias_one,
        up_shift,
        gain_two,
        bias_two,
        conv_shift,
        gain_three,
        bias_three,
        down_shift,
    ) = full_vectors
    up_full = gather_all(up_weight, axes).reshape(-1, inner)
    down_full = gather_all(down_weight.T, axes).reshape(-1, inner)
    conv_all = gather_all(conv_weight.reshape(-1, inner), axes)
    conv_full = conv_all.reshape(devices, KERNEL, taps_in, inner).transpose(1, 0, 2, 3).reshape(KERNEL, -1, inner)
    count = inputs.shape[0]
    reach = KERNEL // 2 * DILATION
    masks = tap_masks(lengths[0], count)
    keep_col = keep_mask.astype(jnp.float32)[:, None]
    x_float = inputs.astype(jnp.float32)
    act_first, back_one = jax.vjp(norm_act, x_float, gain_one, bias_one)
    act_one = act_first.astype(jnp.bfloat16)
    up_out = jnp.dot(act_one, up_full, preferred_element_type=jnp.float32) + up_shift

    def masked_act(field, gain, shift):
        return norm_act(field, gain, shift) * keep_col

    act_second, back_two = jax.vjp(masked_act, up_out, gain_two, bias_two)
    middle = act_second.astype(jnp.bfloat16)
    padded = jnp.pad(middle, ((reach, reach), (0, 0)))
    taps = [
        padded[tap * DILATION : tap * DILATION + count] * masks[tap][:, None].astype(jnp.bfloat16)
        for tap in range(KERNEL)
    ]
    conv_sum = jnp.dot(taps[0], conv_full[0], preferred_element_type=jnp.float32)
    for tap in range(1, KERNEL):
        conv_sum = conv_sum + jnp.dot(taps[tap], conv_full[tap], preferred_element_type=jnp.float32)
    conv_out = conv_sum + conv_shift
    act_third, back_three = jax.vjp(norm_act, conv_out, gain_three, bias_three)
    act_top = act_third.astype(jnp.bfloat16)
    output = (
        x_float + last_dims(act_top, down_full) + down_shift
    ).astype(jnp.bfloat16)
    grad_out = cotangent.astype(jnp.float32)
    down_shift_grad = jnp.sum(grad_out, axis=0)
    down_grad = first_dims(cotangent, act_top)
    top_grad = jnp.dot(cotangent, down_full, preferred_element_type=jnp.float32)
    conv_grad, gain_three_grad, bias_three_grad = back_three(top_grad)
    conv_shift_grad = jnp.sum(conv_grad, axis=0)
    conv_low = conv_grad.astype(jnp.bfloat16)
    conv_grad_weight = jnp.stack([first_dims(tap_in, conv_low) for tap_in in taps])
    padded_grad = jnp.zeros((count + 2 * reach, conv_low.shape[1]), jnp.float32)
    for tap in range(KERNEL):
        term = last_dims(conv_low, conv_full[tap]) * masks[tap][:, None]
        padded_grad = padded_grad.at[tap * DILATION : tap * DILATION + count].add(term)
    middle_grad = padded_grad[reach : reach + count]
    up_grad, gain_two_grad, bias_two_grad = back_two(middle_grad)
    up_shift_grad = jnp.sum(up_grad, axis=0)
    up_low = up_grad.astype(jnp.bfloat16)
    up_grad_weight = first_dims(act_one, up_low)
    act_grad = last_dims(up_low, up_full)
    skip_grad, gain_one_grad, bias_one_grad = back_one(act_grad)
    input_grad = grad_out + skip_grad
    up_own = scatter_all(up_grad_weight.reshape(devices, -1, inner), axes)
    conv_own = scatter_all(
        conv_grad_weight.reshape(KERNEL, devices, taps_in, inner).transpose(1, 0, 2, 3).reshape(devices, -1, inner), axes
    ).reshape(conv_weight.shape)
    down_own = scatter_all(down_grad.reshape(devices, -1, inner), axes).T
    sums = (
        gain_one_grad,
        bias_one_grad,
        up_shift_grad,
        gain_two_grad,
        bias_two_grad,
        conv_shift_grad,
        gain_three_grad,
        bias_three_grad,
        down_shift_grad,
    )
    small_own = scatter_all(
        jnp.concatenate([item.reshape(devices, -1) for item in sums], axis=1)[:, None, :], axes
    )[0]
    owned, at = [up_own, conv_own, down_own], 0
    for width in widths:
        owned.append(small_own[at : at + width])
        at += width
    return (output, input_grad) + tuple(owned)


def solution(mesh):
    rows, columns = mesh.shape["dp"], mesh.shape["fsdp"] // 2
    split = Mesh(mesh.devices.reshape(rows, columns, 2), ALL)
    axes = (("dp", rows), ("chip", columns), ("core", 2))
    in_specs = (
        P(ALL, None),
        P(ALL, None),
        P(ALL),
        P(ALL, None),
        P(ALL),
        P(ALL),
        P(ALL, None),
        P(ALL),
        P(ALL),
        P(ALL),
        P(None, ALL, None),
        P(ALL),
        P(ALL),
        P(ALL),
        P(None, ALL),
        P(ALL),
    )
    out_specs = (
        P(ALL, None),
        P(ALL, None),
        P(ALL, None),
        P(None, ALL, None),
        P(None, ALL),
        P(ALL),
        P(ALL),
        P(ALL),
        P(ALL),
        P(ALL),
        P(ALL),
        P(ALL),
        P(ALL),
        P(ALL),
    )
    return jax.shard_map(functools.partial(body, axes), mesh=split, in_specs=in_specs, out_specs=out_specs, check_vma=False)
```

time: 709 us -> 442 us (0.62)
  waiting for transfers between devices: 336 us -> 68.6 us
  blocking collectives: 82.3 us -> 0 us
  starting transfers between devices: 0.65 us -> 70.4 us
  other arithmetic: 45.5 us -> 92.5 us
  between operations: 15.2 us -> 2.37 us
  local copies, waits for them, and re-layouts: 104 us -> 91.2 us
    unnamed x9 -> x0, waiting for transfers between devices: 328 us -> none
    unnamed x2 -> x0, blocking collectives: 82.3 us -> none
    ppermute x0 -> x56, starting transfers between devices: none -> 70.4 us  [swap(): return lax.ppermute(array, axis, [(k, k ^ mask) for k in range(size)])]
    ppermute x0 -> x56, waiting for transfers between devices: none -> 68.6 us  [swap(): return lax.ppermute(array, axis, [(k, k ^ mask) for k in range(size)])]
    gather x5 -> x0, local copies, waits for them, and re-layouts: 58.9 us -> none  [tap_masks(): matched = segment[jnp.clip(source, 0, count - 1)] == segment]
    another operation x0 -> x14, local copies, waits for them, and re-layouts: none -> 40.7 us  [the longest x6 12.2 us: body(): jnp.stack([first_dims(tap_in, conv_low) for tap_in in taps])]
    unnamed x83 -> x129, local copies, waits for them, and re-layouts: 24.4 us -> 7.94 us
    convert_element_type x9 -> x16, other arithmetic: 0.03 us -> 15 us  [the longest x14 14.9 us: scatter_axis(): arrived = swap(blocks[mask].astype(jnp.bfloat16), axis, size, mask)]
  transfers between devices with their start and end apart: 6 -> 56, of which waited for: 4 -> 21; matrix products, arithmetic and copies ran while one was open for 32% -> 13% of each run, Pallas kernels for 0% -> 0%
where the time goes in v1:
time: 442 us; the launch traced here: 436 us
  matrix products  111 us (25%)
  other arithmetic  92.5 us (21%)
  local copies, waits for them, and re-layouts  91.2 us (21%)
  starting transfers between devices  70.4 us (16%)
  waiting for transfers between devices  68.6 us (16%)
    ppermute x56, starting transfers between devices, swap(): return lax.ppermute(array, axis, [(k, k ^ mask) for k in range(size)])  70.4 us
    ppermute x56, waiting for transfers between devices, swap(): return lax.ppermute(array, axis, [(k, k ^ mask) for k in range(size)])  68.6 us
    dot_general x7, matrix products, last_dims(): lax.dot_general(left, right, (((1,), (1,)), ((), ())), preferred_element_...  37.3 us
    dot_general x7, matrix products, first_dims(): lax.dot_general(left, right, (((0,), (0,)), ((), ())), preferred_element_...  34.8 us
    dot_general x4, matrix products, body(): jnp.dot(taps[tap], conv_full[tap], preferred_element_type=jnp.float32)  20.3 us
    convert_element_type x14, other arithmetic, scatter_axis(): arrived = swap(blocks[mask].astype(jnp.bfloat16), axis, size, mask)  14.9 us
    reduce_sum x2, other arithmetic, norm_act(): return jax.nn.gelu(center * lax.rsqrt(spread + 1e-05) * gain + shift)  14.6 us
    reduce_sum x1, other arithmetic, body(): down_shift_grad = jnp.sum(grad_out, axis=0)  13.6 us
  transfers between devices with their start and end apart: 56, of which 21 were waited for; matrix products, arithmetic and copies ran while one was open for 13% of the time, Pallas kernels for 0%

profile of v1, /device:TPU:0, one launch (start us, length us, event | category | flops | bytes accessed | tf_op | source)
XLA Modules:
  0.0 435.8 jit_solution(14177231443497927004)
XLA Ops:
  0.6 6.1 %concatenate.36 = bf16[240]{0:T(256)(128)(2,1)S(1)} concatenate(bf16[40]{0:T(256)(128)(2,1)} %param.30, bf16[40]{0:T(256)(128)(2,1)} %param.31, bf16[20]{0:T(256)(128)(2,1)} %param.33, bf16[20]{0:T(256)(128)(2,1)} %param.34, bf16[20]{0:T(256)(128)(2,1)} %param.35, bf16[20]{0:T(256)(128)(2,1)} %param.37, bf16[20]{0:T(256)(128)(2,1)} %param.38, bf16[20]{0:T(256)(128)(2,1)} %param.39, ...), dimensions={0} | concatenate | bytes 960 | tf_op jit(solution)/shard_map/concatenate | solution.py:114
  6.8 3.1 collective-permute-start.2
  9.8 2.6 collective-permute-start.1
  13.3 3.5 collective-permute-start.22
  16.9 3.3 convert_reduce_fusion
  27.9 2.4 collective-permute-done.3
  32.2 8.5 %fusion.12 = bf16[2048,1280]{1,0:T(8,128)(2,1)} fusion(bf16[2048,1280]{1,0:T(8,128)(2,1)} %param.26, f32[1280]{0:T(1024)S(1)} %reshape.1009, f32[1280]{0:T(1024)S(1)} %reshape.1008, f32[2048]{0:T(1024)S(1)} %fusion.115, f32[2048]{0:T(1024)S(1)} %broadcast_multiply_fusion.2), kind=kLoop, calls=%fused_computation.20 | loop fusion | flops 36700160 | bytes 10512384 | tf_op jit(solution)/shard_map/convert_element_type | solution.py:140
  45.9 2.2 collective-permute-start.15
  53.9 6.1 %collective-permute-start.11 = (bf16[4,40,640]{2,1,0:T(8,128)(2,1)S(1)}, bf16[4,40,640]{2,1,0:T(8,128)(2,1)S(1)}, u32[]{:S(2)}, u32[]{:S(2)}) collective-permute-start(bf16[4,40,640]{2,1,0:T(8,128)(2,1)S(1)} %pad_maximum_fusion.7), channel_id=1, source_target_pairs={{0,16},{8,24},{16,0},{24,8},{1,17},{9,25},{17,1},{25,9},{2,18},{10... | collective-permute-start | bytes 614408 | tf_op jit(solution)/shard_map/ppermute | solution.py:58
  63.4 10.2 %collective-permute-done.11 = bf16[4,40,640]{2,1,0:T(8,128)(2,1)S(1)} collective-permute-done((bf16[4,40,640]{2,1,0:T(8,128)(2,1)S(1)}, bf16[4,40,640]{2,1,0:T(8,128)(2,1)S(1)}, u32[]{:S(2)}, u32[]{:S(2)}) %collective-permute-start.11) | collective-permute-done | bytes 204832 | tf_op jit(solution)/shard_map/ppermute | solution.py:58
  78.4 7.5 %collective-permute-done.19 = bf16[4,100,640]{2,0,1:T(4,128)(2,1)S(1)} collective-permute-done((bf16[4,100,640]{2,0,1:T(4,128)(2,1)S(1)}, bf16[4,100,640]{2,0,1:T(4,128)(2,1)S(1)}, u32[]{:S(2)}, u32[]{:S(2)}) %collective-permute-start.19) | collective-permute-done | bytes 512032 | tf_op jit(solution)/shard_map/ppermute | solution.py:58
  85.9 7.6 %collective-permute-done.18 = bf16[4,100,640]{2,0,1:T(4,128)(2,1)S(1)} collective-permute-done((bf16[4,100,640]{2,0,1:T(4,128)(2,1)S(1)}, bf16[4,100,640]{2,0,1:T(4,128)(2,1)S(1)}, u32[]{:S(2)}, u32[]{:S(2)}) %collective-permute-start.18) | collective-permute-done | bytes 512032 | tf_op jit(solution)/shard_map/ppermute | solution.py:58
  96.9 4.4 add_reduce_fusion.2
  104.4 4.1 multiply_convert_fusion.1
  110.1 6.2 %copy.365 = bf16[4,4,2,100,640]{4,2,1,0,3:T(2,128)(2,1)} copy(bf16[4,4,2,100,640]{4,3,1,0,2:T(8,128)(2,1)S(1)} %pad_maximum_fusion) | data formatting | bytes 8192000 | tf_op jit(solution)/shard_map/stack | solution.py:63
  116.3 9.4 %reshape_reshape.19 = bf16[32,5,20,640]{3,0,2,1:T(8,128)(2,1)} reshape(bf16[4,4,2,100,640]{4,2,1,0,3:T(2,128)(2,1)} %copy.365) | data formatting | bytes 8192000 | tf_op jit(solution)/shard_map/reshape;reshape | solution.py:133
  125.6 3.8 fusion.156
  131.2 2.5 copy.370
  135.8 2.4 copy.367
  140.2 2.4 copy.366
  142.6 2.5 squeeze.10
  145.1 3.8 fusion.49
  149.0 4.4 %fusion.51 = f32[2048,640]{1,0:T(8,128)} fusion(bf16[640,640]{1,0:T(8,128)(2,1)S(1)} %copy-done.10, bf16[2048]{0:T(1024)(128)(2,1)S(1)} %copy-done.39, bf16[2048,640]{1,0:T(8,128)(2,1)S(1)} %copy-done.6), kind=kOutput, calls=%fused_computation.103 | convolution fusion | flops 1682964480 | bytes 8687616 | tf_op jit(solution)/shard_map/dot_general | solution.py:155
  153.4 4.3 fusion.44
  157.7 4.3 fusion.47
  162.0 7.8 %fusion.158 = (f32[2048]{0:T(1024)S(1)}, f32[2048,640]{1,0:T(8,128)S(1)}) fusion(f32[640]{0:T(1024)S(1)} %copy-done.30, bf16[640,640]{1,0:T(8,128)(2,1)S(1)} %squeeze.14, bf16[2048]{0:T(1024)(128)(2,1)S(1)} %get-tuple-element.94, bf16[2048,640]{1,0:T(8,128)(2,1)S(1)} %copy-done.6, f32[2048,640]{1,0:T(8,128)} %fusion.51, f32[2048,640]{1,0:T(8,128)} %fusion.44, ...), kind=kOutput, calls=%fused_computation.417 | convolution fusion | flops 1690826752 | bytes 29669888 | tf_op jit(solution)/shard_map/dot_general | solution.py:155
  170.7 6.5 %convolution_bitcast_fusion = f32[1280,640]{0,1:T(8,128)} fusion(bf16[2048,1280]{1,0:T(8,128)(2,1)S(1)} %bitcast.410, f32[2048,640]{1,0:T(8,128)S(1)} %get-tuple-element.201, f32[640]{0:T(1024)S(1)} %copy-done.41, f32[640]{0:T(1024)S(1)} %copy-done.28, f32[2048]{0:T(1024)S(1)} %fusion.117, f32[2048]{0:T(1024)S(1)} %broadcast_multiply_fusion), kind=kOutput, calls=%fused_computation.85 | convolution fusion | flops 3372482560 | bytes 13784064 | tf_op jit(solution)/shard_map/dot_general | solution.py:46
  177.2 9.6 %multiply_reduce_fusion = (f32[640]{0:T(1024)}, f32[2048]{0:T(1024)S(1)}, f32[640]{0:T(1024)}, f32[2048,640]{1,0:T(8,128)S(1)}) fusion(f32[2048,640]{1,0:T(8,128)S(1)} %get-tuple-element.201, f32[2048]{0:T(1024)S(1)} %fusion.117, f32[2048]{0:T(1024)S(1)} %broadcast_multiply_fusion, f32[640]{0:T(1024)S(1)} %copy-done.28, f32[640]{0:T(1024)S(1)} %copy-done.41, ...), kind=kOutput, calls=%fused_computation.63 | convolution fusion | flops 3393451008 | bytes 17401856 | tf_op jit(solution)/shard_map/dot_general | solution.py:165
  190.3 3.6 fusion.52
  193.9 3.7 fusion.50
  197.6 3.6 fusion.42
  201.2 3.7 fusion.48
  204.9 3.6 fusion.46
  208.5 2.8 convolution_multiply_fusion
  212.5 2.9 add_dynamic-update-slice_fusion
  215.3 2.9 fusion.37
  218.2 2.9 fusion.36
  221.1 3.1 fusion.35
  224.2 6.7 %multiply_reduce_fusion.1 = (f32[640]{0:T(1024)S(1)}, f32[2048]{0:T(1024)S(1)}, f32[640]{0:T(1024)S(1)}, f32[2048,640]{1,0:T(8,128)S(1)}) fusion(f32[2048]{0:T(1024)S(1)} %fusion.116, f32[2048]{0:T(1024)S(1)} %broadcast_multiply_fusion.1, f32[2048,640]{1,0:T(8,128)S(1)} %bitcast.397, f32[640]{0:T(1024)S(1)} %reshape.1010, f32[640]{0:T(1024)S(1)} %reshape.1011, ...), kind=kLoop, calls=%fused_computation.64 | loop fusion | flops 40628992 | bytes 15774208 | tf_op jit(solution)/shard_map/transpose(jvp())/reduce_sum | solution.py:17
  231.0 2.6 fusion.149
  236.2 14.6 %fusion.148 = (f32[1280]{0:T(1024)S(1)}, f32[2048]{0:T(1024)S(1)}, f32[2048,1280]{1,0:T(8,128)}) fusion(f32[1280]{0:T(1024)S(1)} %reshape.1008, f32[2048]{0:T(1024)S(1)} %broadcast_multiply_fusion.2, bf16[2048,1280]{1,0:T(8,128)(2,1)S(1)} %bitcast.393, f32[1280]{0:T(1024)S(1)} %copy-done.25, f32[2048]{0:T(1024)S(1)} %fusion.115, ...), kind=kOutput, calls=%fused_computation.408 | convolution fusion | flops 3431461632 | bytes 22658048 | tf_op jit(solution)/shard_map/dot_general | solution.py:52
  252.3 2.6 stack.229
  254.9 2.6 stack.228
  257.5 2.7 stack.226
  260.2 2.7 stack.227
  266.8 4.7 %copy.380 = f32[32,5,20,640]{3,0,2,1:T(8,128)} copy(f32[32,5,20,640]{3,2,0,1:T(8,128)S(1)} %bitcast.403) | data formatting | bytes 16384000 | tf_op jit(solution)/shard_map/transpose | solution.py:184
  271.5 10.3 %reshape_reshape.22 = f32[4,4,2,100,640]{4,2,1,0,3:T(2,128)} reshape(f32[32,5,20,640]{3,0,2,1:T(8,128)} %copy.380) | data formatting | bytes 16384000 | tf_op jit(solution)/shard_map/reshape;reshape | solution.py:85
  281.8 12.6 %broadcast_select_fusion.1 = f32[4,4,1,100,640]{4,2,1,0,3:T(1,128)} fusion(pred[]{:T(512)S(6)} %ne.10, f32[4,4,2,100,640]{4,2,1,0,3:T(2,128)} %reshape_reshape.22), kind=kLoop, calls=%fused_computation.32 | loop fusion | flops 1024000 | bytes 12288001 | tf_op jit(solution)/shard_map/jit(_where)/select_n | solution.py:40
  294.5 10.0 %fusion.41 = bf16[4,4,1,100,640]{4,2,1,0,3:T(2,128)(2,1)} fusion(pred[]{:T(512)S(6)} %ne.10, f32[4,4,2,100,640]{4,2,1,0,3:T(2,128)} %reshape_reshape.22), kind=kLoop, calls=%fused_computation.82 | loop fusion | flops 1024000 | bytes 6144001 | tf_op jit(solution)/shard_map/convert_element_type | solution.py:71
  304.6 8.3 %fusion.22 = bf16[2048,1280]{1,0:T(8,128)(2,1)} fusion(bf16[2048,1280]{1,0:T(8,128)(2,1)S(1)} %bitcast.395, bf16[1280,640]{1,0:T(8,128)(2,1)S(1)} %bitcast.412, f32[1280]{0:T(1024)S(1)} %copy-done.32, f32[2048,640]{1,0:T(8,128)S(1)} %bitcast.399, f32[640]{0:T(1024)S(1)} %copy-done.42, f32[640]{0:T(1024)S(1)} %copy-done.29, f32[2048]{0:T(1024)S(1)} %copy-done.27, ...), kind=kOutput, calls=%fused_computation.30 | convolution fusion | flops 3382968320 | bytes 17393664 | tf_op jit(solution)/shard_map/dot_general | solution.py:52
  313.7 7.8 %fusion.15 = (f32[1280]{0:T(1024)S(1)}, f32[2048]{0:T(1024)S(1)}) fusion(f32[2048,1280]{1,0:T(8,128)} %get-tuple-element.203, bf16[2048,1280]{1,0:T(8,128)(2,1)} %param.26, f32[2048]{0:T(1024)S(1)} %fusion.115, f32[2048]{0:T(1024)S(1)} %broadcast_multiply_fusion.2, f32[2048]{0:T(1024)S(1)} %multiply_multiply_fusion.6, f32[1280]{0:T(1024)S(1)} %reshape.1008), kind=kLoop, calls=%fused_computation.23 | loop fusion | flops 28832512 | bytes 15771648 | tf_op jit(solution)/shard_map/transpose(jvp())/reduce_sum | solution.py:17
  321.7 13.6 %convert_reduce_fusion.1 = (f32[1280]{0:T(1024)S(1)}, f32[2048,1280]{1,0:T(8,128)}) fusion(bf16[2048,1280]{1,0:T(8,128)(2,1)} %param.29, f32[2048]{0:T(1024)S(1)} %negate_multiply_fusion, f32[2048]{0:T(1024)S(1)} %multiply_multiply_fusion.6, f32[2048]{0:T(1024)S(1)} %broadcast_multiply_fusion.2, bf16[2048,1280]{1,0:T(8,128)(2,1)} %param.26, ...), kind=kLoop, calls=%fused_computation.10 | loop fusion | flops 28834560 | bytes 31500288 | tf_op jit(solution)/shard_map/reduce_sum | solution.py:163
  335.8 10.1 %fusion.146 = f32[1280,640]{1,0:T(8,128)} fusion(bf16[2048,1280]{1,0:T(8,128)(2,1)} %fusion.12, f32[2048,640]{1,0:T(8,128)} %copy-done.3, f32[2048]{0:T(1024)S(1)} %negate_multiply_fusion.1), kind=kOutput, calls=%fused_computation.406 | convolution fusion | flops 3358064640 | bytes 13770752 | tf_op jit(solution)/shard_map/dot_general | solution.py:46
  345.9 3.6 copy.392
  357.8 5.4 %collective-permute-start.54 = (bf16[1,240]{1,0:T(2,128)(2,1)S(1)}, bf16[1,240]{1,0:T(2,128)(2,1)S(1)}, u32[]{:S(2)}, u32[]{:S(2)}) collective-permute-start(bf16[1,240]{1,0:T(2,128)(2,1)S(1)} %get-tuple-element.183), channel_id=1, source_target_pairs={{0,4},{2,6},{4,0},{6,2},{1,5},{3,7},{5,1},{7,3},{8,12},{10,14},{12... | collective-permute-start | bytes 1448 | tf_op jit(solution)/shard_map/ppermute | solution.py:58
  373.8 3.8 collective-permute-done.43
  382.2 4.2 collective-permute-done.29
  389.2 3.8 collective-permute-start.48
  400.5 3.8 collective-permute-start.34
  407.6 3.7 collective-permute-done.38
  411.3 6.0 %collective-permute-done.36 = bf16[4,100,640]{2,0,1:T(4,128)(2,1)S(1)} collective-permute-done((bf16[4,100,640]{2,0,1:T(4,128)(2,1)S(1)}, bf16[4,100,640]{2,0,1:T(4,128)(2,1)S(1)}, u32[]{:S(2)}, u32[]{:S(2)}) %collective-permute-start.36) | collective-permute-done | bytes 512032 | tf_op jit(solution)/shard_map/ppermute | solution.py:58
  419.4 3.2 collective-permute-start.41
  424.5 3.3 collective-permute-done.41
  427.7 7.1 %collective-permute-done.40 = bf16[100,640]{1,0:T(8,128)(2,1)S(1)} collective-permute-done((bf16[100,640]{1,0:T(8,128)(2,1)S(1)}, bf16[100,640]{1,0:T(8,128)(2,1)S(1)}, u32[]{:S(2)}, u32[]{:S(2)}) %collective-permute-start.40) | collective-permute-done | bytes 128032 | tf_op jit(solution)/shard_map/ppermute | solution.py:58
  (350 shorter events, 99.5 us)
Async XLA Ops:
  6.8 16.0 %collective-permute-start.2 = (bf16[1,240]{1,0:T(2,128)(2,1)S(1)}, bf16[1,240]{1,0:T(2,128)(2,1)S(1)}, u32[]{:S(2)}, u32[]{:S(2)}) collective-permute-start(bf16[1,240]{1,0:T(2,128)(2,1)S(1)} %broadcast_in_dim.30), channel_id=1, source_target_pairs={{0,2},{2,0},{4,6},{6,4},{1,3},{3,1},{5,7},{7,5},{8,10},{10,8},{12,... | collective-permute-start | bytes 1448 | tf_op jit(solution)/shard_map/ppermute | solution.py:58
  9.8 12.9 %collective-permute-start.1 = (bf16[1,240]{1,0:T(2,128)(2,1)S(1)}, bf16[1,240]{1,0:T(2,128)(2,1)S(1)}, u32[]{:S(2)}, u32[]{:S(2)}) collective-permute-start(bf16[1,240]{1,0:T(2,128)(2,1)S(1)} %broadcast_in_dim.30), channel_id=1, source_target_pairs={{0,4},{2,6},{4,0},{6,2},{1,5},{3,7},{5,1},{7,3},{8,12},{10,14},{12... | collective-permute-start | bytes 1448 | tf_op jit(solution)/shard_map/ppermute | solution.py:58
  12.4 10.3 %collective-permute-start = (bf16[1,240]{1,0:T(2,128)(2,1)S(1)}, bf16[1,240]{1,0:T(2,128)(2,1)S(1)}, u32[]{:S(2)}, u32[]{:S(2)}) collective-permute-start(bf16[1,240]{1,0:T(2,128)(2,1)S(1)} %broadcast_in_dim.30), channel_id=1, source_target_pairs={{0,6},{2,4},{4,2},{6,0},{1,7},{3,5},{5,3},{7,1},{8,14},{10,12},{12... | collective-permute-start | bytes 1448 | tf_op jit(solution)/shard_map/ppermute | solution.py:58
  12.4 31.5 %collective-permute-start.23 = (bf16[40,640]{1,0:T(8,128)(2,1)}, bf16[40,640]{1,0:T(8,128)(2,1)S(1)}, u32[]{:S(2)}, u32[]{:S(2)}) collective-permute-start(bf16[40,640]{1,0:T(8,128)(2,1)} %bitcast.418), channel_id=1, source_target_pairs={{0,2},{2,0},{4,6},{6,4},{1,3},{3,1},{5,7},{7,5},{8,10},{10,8},{12,... | collective-permute-start | bytes 153608 | tf_op jit(solution)/shard_map/ppermute | solution.py:58
  13.3 31.4 %collective-permute-start.22 = (bf16[40,640]{1,0:T(8,128)(2,1)}, bf16[40,640]{1,0:T(8,128)(2,1)S(1)}, u32[]{:S(2)}, u32[]{:S(2)}) collective-permute-start(bf16[40,640]{1,0:T(8,128)(2,1)} %bitcast.419), channel_id=1, source_target_pairs={{0,4},{2,6},{4,0},{6,2},{1,5},{3,7},{5,1},{7,3},{8,12},{10,14},{12... | collective-permute-start | bytes 153608 | tf_op jit(solution)/shard_map/ppermute | solution.py:58
  16.9 14.2 %copy-start.33 = (s32[2048]{0:T(1024)S(1)}, s32[2048]{0:T(1024)}, u32[]{:S(2)}) copy-start(s32[2048]{0:T(1024)} %param.28) | copy-start | bytes 24580
  21.7 19.0 %copy-start.20 = (f32[2048]{0:T(1024)}, f32[2048]{0:T(1024)S(1)}, u32[]{:S(2)}) copy-start(f32[2048]{0:T(1024)S(1)} %fusion.19) | copy-start | bytes 24580
  22.8 3.7 collective-permute-start.5
  24.4 3.6 collective-permute-start.4
  25.9 4.5 %collective-permute-start.3 = (bf16[4,1,240]{2,0,1:T(4,128)(2,1)S(1)}, bf16[4,1,240]{2,0,1:T(4,128)(2,1)S(1)}, u32[]{:S(2)}, u32[]{:S(2)}) collective-permute-start(bf16[4,1,240]{2,0,1:T(4,128)(2,1)S(1)} %pad_maximum_fusion.11), channel_id=1, source_target_pairs={{0,24},{8,16},{16,8},{24,0},{1,25},{9,17},{17,9},{25,1},{2,26},{10... | collective-permute-start | bytes 5768 | tf_op jit(solution)/shard_map/ppermute | solution.py:58
  26.5 19.5 %collective-permute-start.21 = (bf16[40,640]{1,0:T(8,128)(2,1)S(1)}, bf16[40,640]{1,0:T(8,128)(2,1)S(1)}, u32[]{:S(2)}, u32[]{:S(2)}) collective-permute-start(bf16[40,640]{1,0:T(8,128)(2,1)S(1)} %bitcast.420), channel_id=1, source_target_pairs={{0,6},{2,4},{4,2},{6,0},{1,7},{3,5},{5,3},{7,1},{8,14},{10,12},{12... | collective-permute-start | bytes 153608 | tf_op jit(solution)/shard_map/ppermute | solution.py:58
  27.9 20.3 %collective-permute-start.8 = (bf16[40,640]{1,0:T(8,128)(2,1)S(1)}, bf16[40,640]{1,0:T(8,128)(2,1)S(1)}, u32[]{:S(2)}, u32[]{:S(2)}) collective-permute-start(bf16[40,640]{1,0:T(8,128)(2,1)S(1)} %copy-done.23), channel_id=1, source_target_pairs={{0,4},{2,6},{4,0},{6,2},{1,5},{3,7},{5,1},{7,3},{8,12},{10,14},{12... | collective-permute-start | bytes 153608 | tf_op jit(solution)/shard_map/ppermute | solution.py:58
  30.4 1.2 collective-permute-start.6
  31.6 18.1 %collective-permute-start.7 = (bf16[40,640]{1,0:T(8,128)(2,1)S(1)}, bf16[40,640]{1,0:T(8,128)(2,1)S(1)}, u32[]{:S(2)}, u32[]{:S(2)}) collective-permute-start(bf16[40,640]{1,0:T(8,128)(2,1)S(1)} %copy-done.23), channel_id=1, source_target_pairs={{0,6},{2,4},{4,2},{6,0},{1,7},{3,5},{5,3},{7,1},{8,14},{10,12},{12... | collective-permute-start | bytes 153608 | tf_op jit(solution)/shard_map/ppermute | solution.py:58
  43.9 6.3 %collective-permute-start.9 = (bf16[40,640]{1,0:T(8,128)(2,1)S(1)}, bf16[40,640]{1,0:T(8,128)(2,1)S(1)}, u32[]{:S(2)}, u32[]{:S(2)}) collective-permute-start(bf16[40,640]{1,0:T(8,128)(2,1)S(1)} %copy-done.23), channel_id=1, source_target_pairs={{0,2},{2,0},{4,6},{6,4},{1,3},{3,1},{5,7},{7,5},{8,10},{10,8},{12,... | collective-permute-start | bytes 153608 | tf_op jit(solution)/shard_map/ppermute | solution.py:58
  44.8 8.3 %collective-permute-start.16 = (bf16[100,640]{1,0:T(8,128)(2,1)S(1)}, bf16[100,640]{1,0:T(8,128)(2,1)S(1)}, u32[]{:S(2)}, u32[]{:S(2)}) collective-permute-start(bf16[100,640]{1,0:T(8,128)(2,1)S(1)} %reshape.1006), channel_id=1, source_target_pairs={{0,2},{2,0},{4,6},{6,4},{1,3},{3,1},{5,7},{7,5},{8,10},{10,8},{12,... | collective-permute-start | bytes 384008 | tf_op jit(solution)/shard_map/ppermute | solution.py:58
  45.9 8.0 %collective-permute-start.15 = (bf16[100,640]{1,0:T(8,128)(2,1)S(1)}, bf16[100,640]{1,0:T(8,128)(2,1)S(1)}, u32[]{:S(2)}, u32[]{:S(2)}) collective-permute-start(bf16[100,640]{1,0:T(8,128)(2,1)S(1)} %reshape.1006), channel_id=1, source_target_pairs={{0,4},{2,6},{4,0},{6,2},{1,5},{3,7},{5,1},{7,3},{8,12},{10,14},{12... | collective-permute-start | bytes 384008 | tf_op jit(solution)/shard_map/ppermute | solution.py:58
  48.2 11.8 %collective-permute-start.14 = (bf16[100,640]{1,0:T(8,128)(2,1)S(1)}, bf16[100,640]{1,0:T(8,128)(2,1)S(1)}, u32[]{:S(2)}, u32[]{:S(2)}) collective-permute-start(bf16[100,640]{1,0:T(8,128)(2,1)S(1)} %reshape.1006), channel_id=1, source_target_pairs={{0,6},{2,4},{4,2},{6,0},{1,7},{3,5},{5,3},{7,1},{8,14},{10,12},{12... | collective-permute-start | bytes 384008 | tf_op jit(solution)/shard_map/ppermute | solution.py:58
  49.7 26.5 %collective-permute-start.26 = (bf16[4,40,640]{2,1,0:T(8,128)(2,1)S(1)}, bf16[4,40,640]{2,1,0:T(8,128)(2,1)S(1)}, u32[]{:S(2)}, u32[]{:S(2)}) collective-permute-start(bf16[4,40,640]{2,1,0:T(8,128)(2,1)S(1)} %pad_maximum_fusion.8), channel_id=1, source_target_pairs={{0,8},{8,0},{16,24},{24,16},{1,9},{9,1},{17,25},{25,17},{2,10},{10... | collective-permute-start | bytes 614408 | tf_op jit(solution)/shard_map/ppermute | solution.py:58
  50.2 27.2 %collective-permute-start.25 = (bf16[4,40,640]{2,1,0:T(8,128)(2,1)S(1)}, bf16[4,40,640]{2,1,0:T(8,128)(2,1)S(1)}, u32[]{:S(2)}, u32[]{:S(2)}) collective-permute-start(bf16[4,40,640]{2,1,0:T(8,128)(2,1)S(1)} %pad_maximum_fusion.8), channel_id=1, source_target_pairs={{0,16},{8,24},{16,0},{24,8},{1,17},{9,25},{17,1},{25,9},{2,18},{10... | collective-permute-start | bytes 614408 | tf_op jit(solution)/shard_map/ppermute | solution.py:58
  53.1 8.7 %collective-permute-start.12 = (bf16[4,40,640]{2,1,0:T(8,128)(2,1)S(1)}, bf16[4,40,640]{2,1,0:T(8,128)(2,1)S(1)}, u32[]{:S(2)}, u32[]{:S(2)}) collective-permute-start(bf16[4,40,640]{2,1,0:T(8,128)(2,1)S(1)} %pad_maximum_fusion.7), channel_id=1, source_target_pairs={{0,8},{8,0},{16,24},{24,16},{1,9},{9,1},{17,25},{25,17},{2,10},{10... | collective-permute-start | bytes 614408 | tf_op jit(solution)/shard_map/ppermute | solution.py:58
  53.9 19.7 %collective-permute-start.11 = (bf16[4,40,640]{2,1,0:T(8,128)(2,1)S(1)}, bf16[4,40,640]{2,1,0:T(8,128)(2,1)S(1)}, u32[]{:S(2)}, u32[]{:S(2)}) collective-permute-start(bf16[4,40,640]{2,1,0:T(8,128)(2,1)S(1)} %pad_maximum_fusion.7), channel_id=1, source_target_pairs={{0,16},{8,24},{16,0},{24,8},{1,17},{9,25},{17,1},{25,9},{2,18},{10... | collective-permute-start | bytes 614408 | tf_op jit(solution)/shard_map/ppermute | solution.py:58
  60.0 15.0 %collective-permute-start.10 = (bf16[4,40,640]{2,1,0:T(8,128)(2,1)S(1)}, bf16[4,40,640]{2,1,0:T(8,128)(2,1)S(1)}, u32[]{:S(2)}, u32[]{:S(2)}) collective-permute-start(bf16[4,40,640]{2,1,0:T(8,128)(2,1)S(1)} %pad_maximum_fusion.7), channel_id=1, source_target_pairs={{0,24},{8,16},{16,8},{24,0},{1,25},{9,17},{17,9},{25,1},{2,26},{10... | collective-permute-start | bytes 614408 | tf_op jit(solution)/shard_map/ppermute | solution.py:58
  61.8 15.7 %collective-permute-start.24 = (bf16[4,40,640]{2,1,0:T(8,128)(2,1)S(1)}, bf16[4,40,640]{2,1,0:T(8,128)(2,1)S(1)}, u32[]{:S(2)}, u32[]{:S(2)}) collective-permute-start(bf16[4,40,640]{2,1,0:T(8,128)(2,1)S(1)} %pad_maximum_fusion.8), channel_id=1, source_target_pairs={{0,24},{8,16},{16,8},{24,0},{1,25},{9,17},{17,9},{25,1},{2,26},{10... | collective-permute-start | bytes 614408 | tf_op jit(solution)/shard_map/ppermute | solution.py:58
  73.6 12.3 %collective-permute-start.19 = (bf16[4,100,640]{2,0,1:T(4,128)(2,1)S(1)}, bf16[4,100,640]{2,0,1:T(4,128)(2,1)S(1)}, u32[]{:S(2)}, u32[]{:S(2)}) collective-permute-start(bf16[4,100,640]{2,0,1:T(4,128)(2,1)S(1)} %copy.353), channel_id=1, source_target_pairs={{0,8},{8,0},{16,24},{24,16},{1,9},{9,1},{17,25},{25,17},{2,10},{10... | collective-permute-start | bytes 1536008 | tf_op jit(solution)/shard_map/ppermute | solution.py:58
  75.0 18.5 %collective-permute-start.18 = (bf16[4,100,640]{2,0,1:T(4,128)(2,1)S(1)}, bf16[4,100,640]{2,0,1:T(4,128)(2,1)S(1)}, u32[]{:S(2)}, u32[]{:S(2)}) collective-permute-start(bf16[4,100,640]{2,0,1:T(4,128)(2,1)S(1)} %copy.353), channel_id=1, source_target_pairs={{0,16},{8,24},{16,0},{24,8},{1,17},{9,25},{17,1},{25,9},{2,18},{10... | collective-permute-start | bytes 1536008 | tf_op jit(solution)/shard_map/ppermute | solution.py:58
  76.2 17.2 %collective-permute-start.17 = (bf16[4,100,640]{2,0,1:T(4,128)(2,1)S(1)}, bf16[4,100,640]{2,0,1:T(4,128)(2,1)S(1)}, u32[]{:S(2)}, u32[]{:S(2)}) collective-permute-start(bf16[4,100,640]{2,0,1:T(4,128)(2,1)S(1)} %copy.353), channel_id=1, source_target_pairs={{0,24},{8,16},{16,8},{24,0},{1,25},{9,17},{17,9},{25,1},{2,26},{10... | collective-permute-start | bytes 1536008 | tf_op jit(solution)/shard_map/ppermute | solution.py:58
  77.5 18.1 %collective-permute-start.13 = (bf16[4,4,40,640]{3,2,1,0:T(8,128)(2,1)S(1)}, bf16[4,4,40,640]{3,2,1,0:T(8,128)(2,1)S(1)}, u32[]{:S(2)}, u32[]{:S(2)}) collective-permute-start(bf16[4,4,40,640]{3,2,1,0:T(8,128)(2,1)S(1)} %pad_maximum_fusion.4), channel_id=1, source_target_pairs={{0,1},{1,0},{2,3},{3,2},{4,5},{5,4},{6,7},{7,6},{8,9},{9,8},{10,11... | collective-permute-start | bytes 2457608 | tf_op jit(solution)/shard_map/ppermute | solution.py:58
  77.8 23.4 %collective-permute-start.27 = (bf16[4,4,40,640]{3,2,1,0:T(8,128)(2,1)S(1)}, bf16[4,4,40,640]{3,2,1,0:T(8,128)(2,1)S(1)}, u32[]{:S(2)}, u32[]{:S(2)}) collective-permute-start(bf16[4,4,40,640]{3,2,1,0:T(8,128)(2,1)S(1)} %pad_maximum_fusion.5), channel_id=1, source_target_pairs={{0,1},{1,0},{2,3},{3,2},{4,5},{5,4},{6,7},{7,6},{8,9},{9,8},{10,11... | collective-permute-start | bytes 2457608 | tf_op jit(solution)/shard_map/ppermute | solution.py:58
  95.5 13.0 %collective-permute-start.20 = (bf16[4,4,100,640]{3,1,2,0:T(4,128)(2,1)S(1)}, bf16[4,4,100,640]{3,1,2,0:T(4,128)(2,1)S(1)}, u32[]{:S(2)}, u32[]{:S(2)}) collective-permute-start(bf16[4,4,100,640]{3,1,2,0:T(4,128)(2,1)S(1)} %copy.362), channel_id=1, source_target_pairs={{0,1},{1,0},{2,3},{3,2},{4,5},{5,4},{6,7},{7,6},{8,9},{9,8},{10,11... | collective-permute-start | bytes 6144008 | tf_op jit(solution)/shard_map/ppermute | solution.py:58
  169.8 17.1 %copy-start.2 = (f32[2048,640]{1,0:T(8,128)}, f32[2048,640]{1,0:T(8,128)S(1)}, u32[]{:S(2)}) copy-start(f32[2048,640]{1,0:T(8,128)S(1)} %get-tuple-element.201) | copy-start | bytes 15728644
  170.7 16.2 %copy-start.26 = (f32[2048]{0:T(1024)}, f32[2048]{0:T(1024)S(1)}, u32[]{:S(2)}) copy-start(f32[2048]{0:T(1024)S(1)} %fusion.117) | copy-start | bytes 24580
  281.8 22.7 %slice-start.2 = ((s8[5242880]{0:T(1024)(128)(4,1)}), s8[4194304]{0:T(1024)(128)(4,1)S(1)}, s32[]{:S(2)}) async-start(s8[5242880]{0:T(1024)(128)(4,1)} %bitcast.394), calls=%async_computation.2 | async-start | bytes 8388608
  281.8 22.7 %slice-start.6 = ((s8[5242880]{0:T(1024)(128)(4,1)}), s8[4194304]{0:T(1024)(128)(4,1)S(1)}, s32[]{:S(2)}) async-start(s8[5242880]{0:T(1024)(128)(4,1)} %bitcast.398), calls=%async_computation.6 | async-start | bytes 8388608
  335.7 13.8 %collective-permute-start.49 = (bf16[4,4,1,240]{3,2,1,0:T(2,128)(2,1)S(1)}, bf16[4,4,1,240]{3,2,1,0:T(2,128)(2,1)S(1)}, u32[]{:S(2)}, u32[]{:S(2)}) collective-permute-start(bf16[4,4,1,240]{3,2,1,0:T(2,128)(2,1)S(1)} %fusion.113), channel_id=1, source_target_pairs={{0,1},{1,0},{2,3},{3,2},{4,5},{5,4},{6,7},{7,6},{8,9},{9,8},{10,11... | collective-permute-start | bytes 23048 | tf_op jit(solution)/shard_map/ppermute | solution.py:58
  349.6 15.8 %copy-start.5 = (bf16[4,4,1,100,640]{4,2,1,0,3:T(2,128)(2,1)S(1)}, bf16[4,4,1,100,640]{4,2,1,0,3:T(2,128)(2,1)}, u32[]{:S(2)}) copy-start(bf16[4,4,1,100,640]{4,2,1,0,3:T(2,128)(2,1)} %fusion.41) | copy-start | bytes 6144004
  349.7 4.5 %collective-permute-start.52 = (bf16[4,1,240]{2,0,1:T(4,128)(2,1)S(1)}, bf16[4,1,240]{2,0,1:T(4,128)(2,1)S(1)}, u32[]{:S(2)}, u32[]{:S(2)}) collective-permute-start(bf16[4,1,240]{2,0,1:T(4,128)(2,1)S(1)} %bitcast.422), channel_id=1, source_target_pairs={{0,24},{8,16},{16,8},{24,0},{1,25},{9,17},{17,9},{25,1},{2,26},{10... | collective-permute-start | bytes 5768 | tf_op jit(solution)/shard_map/ppermute | solution.py:58
  351.5 3.6 collective-permute-start.51
  352.7 3.6 collective-permute-start.50
  353.5 15.7 %collective-permute-start.42 = (bf16[4,4,40,640]{3,2,1,0:T(8,128)(2,1)S(1)}, bf16[4,4,40,640]{3,2,1,0:T(8,128)(2,1)S(1)}, u32[]{:S(2)}, u32[]{:S(2)}) collective-permute-start(bf16[4,4,40,640]{3,2,1,0:T(8,128)(2,1)S(1)} %fusion.72), channel_id=1, source_target_pairs={{0,1},{1,0},{2,3},{3,2},{4,5},{5,4},{6,7},{7,6},{8,9},{9,8},{10,11... | collective-permute-start | bytes 2457608 | tf_op jit(solution)/shard_map/ppermute | solution.py:58
  356.3 11.1 %collective-permute-start.53 = (bf16[1,240]{1,0:T(2,128)(2,1)S(1)}, bf16[1,240]{1,0:T(2,128)(2,1)S(1)}, u32[]{:S(2)}, u32[]{:S(2)}) collective-permute-start(bf16[1,240]{1,0:T(2,128)(2,1)S(1)} %get-tuple-element.182), channel_id=1, source_target_pairs={{0,2},{2,0},{4,6},{6,4},{1,3},{3,1},{5,7},{7,5},{8,10},{10,8},{12,... | collective-permute-start | bytes 1448 | tf_op jit(solution)/shard_map/ppermute | solution.py:58
  357.8 10.1 %collective-permute-start.54 = (bf16[1,240]{1,0:T(2,128)(2,1)S(1)}, bf16[1,240]{1,0:T(2,128)(2,1)S(1)}, u32[]{:S(2)}, u32[]{:S(2)}) collective-permute-start(bf16[1,240]{1,0:T(2,128)(2,1)S(1)} %get-tuple-element.183), channel_id=1, source_target_pairs={{0,4},{2,6},{4,0},{6,2},{1,5},{3,7},{5,1},{7,3},{8,12},{10,14},{12... | collective-permute-start | bytes 1448 | tf_op jit(solution)/shard_map/ppermute | solution.py:58
  363.2 5.4 %collective-permute-start.55 = (bf16[1,240]{1,0:T(2,128)(2,1)S(1)}, bf16[1,240]{1,0:T(2,128)(2,1)S(1)}, u32[]{:S(2)}, u32[]{:S(2)}) collective-permute-start(bf16[1,240]{1,0:T(2,128)(2,1)S(1)} %get-tuple-element.184), channel_id=1, source_target_pairs={{0,6},{2,4},{4,2},{6,0},{1,7},{3,5},{5,3},{7,1},{8,14},{10,12},{12... | collective-permute-start | bytes 1448 | tf_op jit(solution)/shard_map/ppermute | solution.py:58
  365.3 7.8 %collective-permute-start.28 = (bf16[4,4,40,640]{3,2,1,0:T(8,128)(2,1)S(1)}, bf16[4,4,40,640]{3,2,1,0:T(8,128)(2,1)S(1)}, u32[]{:S(2)}, u32[]{:S(2)}) collective-permute-start(bf16[4,4,40,640]{3,2,1,0:T(8,128)(2,1)S(1)} %fusion.71), channel_id=1, source_target_pairs={{0,1},{1,0},{2,3},{3,2},{4,5},{5,4},{6,7},{7,6},{8,9},{9,8},{10,11... | collective-permute-start | bytes 2457608 | tf_op jit(solution)/shard_map/ppermute | solution.py:58
  367.4 25.9 %collective-permute-start.35 = (bf16[4,4,100,640]{3,1,0,2:T(4,128)(2,1)S(1)}, bf16[4,4,100,640]{3,1,0,2:T(4,128)(2,1)S(1)}, u32[]{:S(2)}, u32[]{:S(2)}) collective-permute-start(bf16[4,4,100,640]{3,1,0,2:T(4,128)(2,1)S(1)} %copy.382), channel_id=1, source_target_pairs={{0,1},{1,0},{2,3},{3,2},{4,5},{5,4},{6,7},{7,6},{8,9},{9,8},{10,11... | collective-permute-start | bytes 6144008 | tf_op jit(solution)/shard_map/ppermute | solution.py:58
  369.5 8.1 %collective-permute-start.43 = (bf16[4,40,640]{2,1,0:T(8,128)(2,1)S(1)}, bf16[4,40,640]{2,1,0:T(8,128)(2,1)S(1)}, u32[]{:S(2)}, u32[]{:S(2)}) collective-permute-start(bf16[4,40,640]{2,1,0:T(8,128)(2,1)S(1)} %get-tuple-element.118), channel_id=1, source_target_pairs={{0,8},{8,0},{16,24},{24,16},{1,9},{9,1},{17,25},{25,17},{2,10},{10... | collective-permute-start | bytes 614408 | tf_op jit(solution)/shard_map/ppermute | solution.py:58
  369.9 10.1 %collective-permute-start.44 = (bf16[4,40,640]{2,1,0:T(8,128)(2,1)S(1)}, bf16[4,40,640]{2,1,0:T(8,128)(2,1)S(1)}, u32[]{:S(2)}, u32[]{:S(2)}) collective-permute-start(bf16[4,40,640]{2,1,0:T(8,128)(2,1)S(1)} %get-tuple-element.119), channel_id=1, source_target_pairs={{0,16},{8,24},{16,0},{24,8},{1,17},{9,25},{17,1},{25,9},{2,18},{10... | collective-permute-start | bytes 614408 | tf_op jit(solution)/shard_map/ppermute | solution.py:58
  371.3 22.0 %copy-start.4 = (f32[4,4,1,100,640]{4,2,1,0,3:T(1,128)S(1)}, f32[4,4,1,100,640]{4,2,1,0,3:T(1,128)}, u32[]{:S(2)}) copy-start(f32[4,4,1,100,640]{4,2,1,0,3:T(1,128)} %broadcast_select_fusion.1) | copy-start | bytes 12288004
  371.3 10.6 %collective-permute-start.45 = (bf16[4,40,640]{2,1,0:T(8,128)(2,1)S(1)}, bf16[4,40,640]{2,1,0:T(8,128)(2,1)S(1)}, u32[]{:S(2)}, u32[]{:S(2)}) collective-permute-start(bf16[4,40,640]{2,1,0:T(8,128)(2,1)S(1)} %get-tuple-element.120), channel_id=1, source_target_pairs={{0,24},{8,16},{16,8},{24,0},{1,25},{9,17},{17,9},{25,1},{2,26},{10... | collective-permute-start | bytes 614408 | tf_op jit(solution)/shard_map/ppermute | solution.py:58
  373.4 13.0 %collective-permute-start.29 = (bf16[4,40,640]{2,1,0:T(8,128)(2,1)S(1)}, bf16[4,40,640]{2,1,0:T(8,128)(2,1)S(1)}, u32[]{:S(2)}, u32[]{:S(2)}) collective-permute-start(bf16[4,40,640]{2,1,0:T(8,128)(2,1)S(1)} %get-tuple-element.121), channel_id=1, source_target_pairs={{0,8},{8,0},{16,24},{24,16},{1,9},{9,1},{17,25},{25,17},{2,10},{10... | collective-permute-start | bytes 614408 | tf_op jit(solution)/shard_map/ppermute | solution.py:58
  377.6 11.6 %collective-permute-start.30 = (bf16[4,40,640]{2,1,0:T(8,128)(2,1)S(1)}, bf16[4,40,640]{2,1,0:T(8,128)(2,1)S(1)}, u32[]{:S(2)}, u32[]{:S(2)}) collective-permute-start(bf16[4,40,640]{2,1,0:T(8,128)(2,1)S(1)} %get-tuple-element.122), channel_id=1, source_target_pairs={{0,16},{8,24},{16,0},{24,8},{1,17},{9,25},{17,1},{25,9},{2,18},{10... | collective-permute-start | bytes 614408 | tf_op jit(solution)/shard_map/ppermute | solution.py:58
  380.0 13.1 %collective-permute-start.31 = (bf16[4,40,640]{2,1,0:T(8,128)(2,1)S(1)}, bf16[4,40,640]{2,1,0:T(8,128)(2,1)S(1)}, u32[]{:S(2)}, u32[]{:S(2)}) collective-permute-start(bf16[4,40,640]{2,1,0:T(8,128)(2,1)S(1)} %get-tuple-element.123), channel_id=1, source_target_pairs={{0,24},{8,16},{16,8},{24,0},{1,25},{9,17},{17,9},{25,1},{2,26},{10... | collective-permute-start | bytes 614408 | tf_op jit(solution)/shard_map/ppermute | solution.py:58
  382.1 15.2 %collective-permute-start.46 = (bf16[40,640]{1,0:T(8,128)(2,1)S(1)}, bf16[40,640]{1,0:T(8,128)(2,1)S(1)}, u32[]{:S(2)}, u32[]{:S(2)}) collective-permute-start(bf16[40,640]{1,0:T(8,128)(2,1)S(1)} %get-tuple-element.141), channel_id=1, source_target_pairs={{0,2},{2,0},{4,6},{6,4},{1,3},{3,1},{5,7},{7,5},{8,10},{10,8},{12,... | collective-permute-start | bytes 153608 | tf_op jit(solution)/shard_map/ppermute | solution.py:58
  386.4 11.2 %collective-permute-start.47 = (bf16[40,640]{1,0:T(8,128)(2,1)S(1)}, bf16[40,640]{1,0:T(8,128)(2,1)S(1)}, u32[]{:S(2)}, u32[]{:S(2)}) collective-permute-start(bf16[40,640]{1,0:T(8,128)(2,1)S(1)} %get-tuple-element.142), channel_id=1, source_target_pairs={{0,4},{2,6},{4,0},{6,2},{1,5},{3,7},{5,1},{7,3},{8,12},{10,14},{12... | collective-permute-start | bytes 153608 | tf_op jit(solution)/shard_map/ppermute | solution.py:58
  389.2 10.7 %collective-permute-start.48 = (bf16[40,640]{1,0:T(8,128)(2,1)S(1)}, bf16[40,640]{1,0:T(8,128)(2,1)S(1)}, u32[]{:S(2)}, u32[]{:S(2)}) collective-permute-start(bf16[40,640]{1,0:T(8,128)(2,1)S(1)} %get-tuple-element.143), channel_id=1, source_target_pairs={{0,6},{2,4},{4,2},{6,0},{1,7},{3,5},{5,3},{7,1},{8,14},{10,12},{12... | collective-permute-start | bytes 153608 | tf_op jit(solution)/shard_map/ppermute | solution.py:58
  393.2 7.2 %collective-permute-start.32 = (bf16[40,640]{1,0:T(8,128)(2,1)S(1)}, bf16[40,640]{1,0:T(8,128)(2,1)S(1)}, u32[]{:S(2)}, u32[]{:S(2)}) collective-permute-start(bf16[40,640]{1,0:T(8,128)(2,1)S(1)} %get-tuple-element.144), channel_id=1, source_target_pairs={{0,2},{2,0},{4,6},{6,4},{1,3},{3,1},{5,7},{7,5},{8,10},{10,8},{12,... | collective-permute-start | bytes 153608 | tf_op jit(solution)/shard_map/ppermute | solution.py:58
  395.8 15.6 %collective-permute-start.38 = (bf16[4,100,640]{2,0,1:T(4,128)(2,1)S(1)}, bf16[4,100,640]{2,0,1:T(4,128)(2,1)S(1)}, u32[]{:S(2)}, u32[]{:S(2)}) collective-permute-start(bf16[4,100,640]{2,0,1:T(4,128)(2,1)S(1)} %fusion.83), channel_id=1, source_target_pairs={{0,24},{8,16},{16,8},{24,0},{1,25},{9,17},{17,9},{25,1},{2,26},{10... | collective-permute-start | bytes 1536008 | tf_op jit(solution)/shard_map/ppermute | solution.py:58
  397.2 20.1 %collective-permute-start.36 = (bf16[4,100,640]{2,0,1:T(4,128)(2,1)S(1)}, bf16[4,100,640]{2,0,1:T(4,128)(2,1)S(1)}, u32[]{:S(2)}, u32[]{:S(2)}) collective-permute-start(bf16[4,100,640]{2,0,1:T(4,128)(2,1)S(1)} %get-tuple-element.108), channel_id=1, source_target_pairs={{0,8},{8,0},{16,24},{24,16},{1,9},{9,1},{17,25},{25,17},{2,10},{10... | collective-permute-start | bytes 1536008 | tf_op jit(solution)/shard_map/ppermute | solution.py:58
  397.6 19.8 %collective-permute-start.37 = (bf16[4,100,640]{2,0,1:T(4,128)(2,1)S(1)}, bf16[4,100,640]{2,0,1:T(4,128)(2,1)S(1)}, u32[]{:S(2)}, u32[]{:S(2)}) collective-permute-start(bf16[4,100,640]{2,0,1:T(4,128)(2,1)S(1)} %get-tuple-element.109), channel_id=1, source_target_pairs={{0,16},{8,24},{16,0},{24,8},{1,17},{9,25},{17,1},{25,9},{2,18},{10... | collective-permute-start | bytes 1536008 | tf_op jit(solution)/shard_map/ppermute | solution.py:58
  399.9 5.0 %collective-permute-start.33 = (bf16[40,640]{1,0:T(8,128)(2,1)S(1)}, bf16[40,640]{1,0:T(8,128)(2,1)S(1)}, u32[]{:S(2)}, u32[]{:S(2)}) collective-permute-start(bf16[40,640]{1,0:T(8,128)(2,1)S(1)} %get-tuple-element.145), channel_id=1, source_target_pairs={{0,4},{2,6},{4,0},{6,2},{1,5},{3,7},{5,1},{7,3},{8,12},{10,14},{12... | collective-permute-start | bytes 153608 | tf_op jit(solution)/shard_map/ppermute | solution.py:58
  400.5 6.5 %collective-permute-start.34 = (bf16[40,640]{1,0:T(8,128)(2,1)S(1)}, bf16[40,640]{1,0:T(8,128)(2,1)S(1)}, u32[]{:S(2)}, u32[]{:S(2)}) collective-permute-start(bf16[40,640]{1,0:T(8,128)(2,1)S(1)} %get-tuple-element.146), channel_id=1, source_target_pairs={{0,6},{2,4},{4,2},{6,0},{1,7},{3,5},{5,3},{7,1},{8,14},{10,12},{12... | collective-permute-start | bytes 153608 | tf_op jit(solution)/shard_map/ppermute | solution.py:58
  419.4 8.3 %collective-permute-start.41 = (bf16[100,640]{1,0:T(8,128)(2,1)S(1)}, bf16[100,640]{1,0:T(8,128)(2,1)S(1)}, u32[]{:S(2)}, u32[]{:S(2)}) collective-permute-start(bf16[100,640]{1,0:T(8,128)(2,1)S(1)} %bitcast.417), channel_id=1, source_target_pairs={{0,6},{2,4},{4,2},{6,0},{1,7},{3,5},{5,3},{7,1},{8,14},{10,12},{12... | collective-permute-start | bytes 384008 | tf_op jit(solution)/shard_map/ppermute | solution.py:58
  422.6 12.3 %collective-permute-start.40 = (bf16[100,640]{1,0:T(8,128)(2,1)S(1)}, bf16[100,640]{1,0:T(8,128)(2,1)S(1)}, u32[]{:S(2)}, u32[]{:S(2)}) collective-permute-start(bf16[100,640]{1,0:T(8,128)(2,1)S(1)} %bitcast.416), channel_id=1, source_target_pairs={{0,4},{2,6},{4,0},{6,2},{1,5},{3,7},{5,1},{7,3},{8,12},{10,14},{12... | collective-permute-start | bytes 384008 | tf_op jit(solution)/shard_map/ppermute | solution.py:58
  422.9 11.9 %collective-permute-start.39 = (bf16[100,640]{1,0:T(8,128)(2,1)S(1)}, bf16[100,640]{1,0:T(8,128)(2,1)S(1)}, u32[]{:S(2)}, u32[]{:S(2)}) collective-permute-start(bf16[100,640]{1,0:T(8,128)(2,1)S(1)} %bitcast.415), channel_id=1, source_target_pairs={{0,2},{2,0},{4,6},{6,4},{1,3},{3,1},{5,7},{7,5},{8,10},{10,8},{12,... | collective-permute-start | bytes 384008 | tf_op jit(solution)/shard_map/ppermute | solution.py:58
  (52 other events, 326.1 us)

commit v2 on v0

v2 whole, which is shorter than its diff:
```python
import functools

import jax
import jax.numpy as jnp
from jax import lax
from jax.experimental import pallas as pl
from jax.experimental.pallas import tpu as pltpu
from jax.sharding import Mesh
from jax.sharding import PartitionSpec as P

KERNEL = 5
DILATION = 8
REACH = KERNEL // 2 * DILATION
ALL = ("dp", "chip", "core")
F32 = jnp.float32
BF16 = jnp.bfloat16
TANH_ONE = 0.7978845608028654
TANH_THREE = TANH_ONE * 0.044715
ROWS = 16
VMEM_BYTES = 56 * 2**20


def xor_order(items, me):
    bit = 1
    while bit < len(items):
        there = (me & bit) != 0
        items = [jnp.where(there, items[k ^ bit], items[k]) for k in range(len(items))]
        bit *= 2
    return items


def swap(array, axis, size, mask):
    return lax.ppermute(array, axis, [(k, k ^ mask) for k in range(size)])


def gather_axis(array, axis, size, place):
    held = [array] + [swap(array, axis, size, mask) for mask in range(1, size)]
    return jnp.stack(xor_order(held, lax.axis_index(axis)), place)


def gather_all(block, axes, order=(1, 0, 2)):
    out, held = block, []
    for axis in order:
        held = sorted(held + [axis])
        out = gather_axis(out, axes[axis][0], axes[axis][1], held.index(axis))
    return out.reshape((-1,) + block.shape)


def scatter_axis(total, axis, size):
    arrived = [swap(total[mask].astype(BF16), axis, size, mask) for mask in range(1, size)]
    kept = total[0].astype(F32)
    for item in arrived:
        kept = kept + item.astype(F32)
    return kept


def scatter_all(kept, sent, axes, order=(0, 1)):
    total = kept.astype(F32) + swap(sent, axes[2][0], axes[2][1], 1).astype(F32)
    if order == (1, 0):
        total = jnp.swapaxes(total, 0, 1)
    for axis in order:
        total = scatter_axis(total, axes[axis][0], axes[axis][1])
    return total


def scatter_exact(kept, sent, axes):
    total = kept + swap(sent, axes[2][0], axes[2][1], 1)
    for axis in (0, 1):
        name, size = axes[axis]
        total = total[0] + sum(swap(total[mask], name, size, mask) for mask in range(1, size))
    return total


def norm(z, width):
    center = z - jnp.sum(z, axis=1, keepdims=True) * (1.0 / width)
    scale = lax.rsqrt(jnp.sum(center * center, axis=1, keepdims=True) * (1.0 / width) + 1e-05)
    return center * scale, scale


def gelu(s):
    square = s * s
    half = 0.5 * s
    return half + half * jnp.tanh(s * (TANH_ONE + TANH_THREE * square))


def gelu_slope(s):
    square = s * s
    t = jnp.tanh(s * (TANH_ONE + TANH_THREE * square))
    return (0.5 + 0.5 * t) + (0.5 * s) * (1.0 - t * t) * (TANH_ONE + 3.0 * TANH_THREE * square)


def norm_back(hat, scale, gain, slope, grad, width):
    by_sum = slope * grad
    by_gain = by_sum * hat
    by_hat = by_sum * gain
    first = jnp.sum(by_hat, axis=1, keepdims=True) * (1.0 / width)
    second = jnp.sum(by_hat * hat, axis=1, keepdims=True) * (1.0 / width)
    return scale * (by_hat - first - hat * second), by_gain, by_sum


def fold(value):
    return value[0:8] + value[8:16]


def chunks(count, body, unroll=4):
    def step(k, carry):
        body(pl.multiple_of(k * ROWS, ROWS))
        return carry

    lax.fori_loop(0, count // ROWS, step, 0, unroll=unroll)


def dot(left, right, left_dim=1, right_dim=0):
    return lax.dot_general(
        left, right, (((left_dim,), (right_dim,)), ((), ())), preferred_element_type=F32
    )


def first_act_kernel(small_ref, x_ref, act_ref, wide_ref, narrow_ref):
    block, width = x_ref.shape

    @pl.when(pl.program_id(0) == 0)
    def _():
        devices = small_ref.shape[0]
        of_wide, of_narrow = width // devices, narrow_ref.shape[1] // devices
        for k in range(devices):
            item = small_ref[k].astype(F32)
            wide_ref[:, k * of_wide : (k + 1) * of_wide] = item[0:8, 0:of_wide]
            narrow_ref[:, k * of_narrow : (k + 1) * of_narrow] = item[8:16, 0:of_narrow]

    gain, bias = wide_ref[0:1, :], wide_ref[1:2, :]

    def body(at):
        hat, _ = norm(x_ref[pl.ds(at, ROWS), :].astype(F32), width)
        act_ref[pl.ds(at, ROWS), :] = gelu(hat * gain + bias).astype(BF16)

    chunks(block, body)


def up_kernel(act_ref, weight_ref, narrow_ref, flags_ref, out_ref, mid_ref):
    block, width = out_ref.shape
    out_ref[...] = dot(act_ref[...], weight_ref[...])
    shift, gain, bias = narrow_ref[0:1, :], narrow_ref[1:2, :], narrow_ref[2:3, :]

    def body(at):
        rows = pl.ds(at, ROWS)
        z = out_ref[rows, :] + shift
        out_ref[rows, :] = z
        hat, _ = norm(z, width)
        mid_ref[rows, :] = (gelu(hat * gain + bias) * flags_ref[rows, 0:1]).astype(BF16)

    chunks(block, body)


def fill_padded(padded_ref, source_ref):
    count, width = source_ref.shape
    padded_ref[0:REACH, :] = jnp.zeros((REACH, width), F32)
    padded_ref[count + REACH : count + 2 * REACH, :] = jnp.zeros((REACH, width), F32)

    def body(at):
        padded_ref[pl.ds(REACH + at, ROWS), :] = source_ref[pl.ds(at, ROWS), :].astype(F32)

    chunks(count, body)


def shifted(padded_ref, flags_ref, start, block, tap):
    at = pl.multiple_of(start + tap * DILATION, DILATION)
    rows = padded_ref[pl.ds(at, block), :]
    if tap != KERNEL // 2:
        rows = rows * flags_ref[:, tap + 1 : tap + 2]
    return rows.astype(BF16)


def conv_kernel(
    mid_ref, pieces_ref, down_ref, cot_ref, narrow_ref, flags_ref, place_ref,
    top_ref, low_ref, weight_ref, sums_ref, wide_sums_ref, kept_ref, sent_ref,
    padded_ref, wide_weight_ref, row_ref, out_ref, grad_ref, down_grad_ref,
):
    step, steps = pl.program_id(0), pl.num_programs(0)
    block, width = out_ref.shape
    devices = pieces_ref.shape[0]
    share = width // devices

    @pl.when(step == 0)
    def _():
        fill_padded(padded_ref, mid_ref)
        for k in range(devices):
            row_ref[...] = pieces_ref[k].astype(F32)
            for tap in range(KERNEL):
                wide_weight_ref[tap, k * share : (k + 1) * share, :] = row_ref[tap * share : (tap + 1) * share, :]
        for tap in range(KERNEL):
            weight_ref[tap] = wide_weight_ref[tap].astype(BF16)
        sums_ref[...] = jnp.zeros_like(sums_ref)
        wide_sums_ref[...] = jnp.zeros_like(wide_sums_ref)
        down_grad_ref[...] = jnp.zeros_like(down_grad_ref)

    start = step * block
    for tap in range(KERNEL):
        term = dot(shifted(padded_ref, flags_ref, start, block, tap), weight_ref[tap])
        out_ref[...] = term if tap == 0 else out_ref[...] + term
    grad_ref[...] = dot(cot_ref[...], down_ref[...])
    shift, gain, bias = narrow_ref[3:4, :], narrow_ref[4:5, :], narrow_ref[5:6, :]

    def body(at):
        rows = pl.ds(at, ROWS)
        hat, scale = norm(out_ref[rows, :] + shift, width)
        s = hat * gain + bias
        square = s * s
        t = jnp.tanh(s * (TANH_ONE + TANH_THREE * square))
        half = 0.5 * s
        top_ref[rows, :] = (half + half * t).astype(BF16)
        slope = (0.5 + 0.5 * t) + half * (1.0 - t * t) * (TANH_ONE + 3.0 * TANH_THREE * square)
        back, by_gain, by_sum = norm_back(hat, scale, gain, slope, grad_ref[rows, :], width)
        low_ref[rows, :] = back.astype(BF16)
        sums_ref[0:8, :] += fold(by_gain)
        sums_ref[8:16, :] += fold(by_sum)
        sums_ref[16:24, :] += fold(back)
        wide_sums_ref[...] += fold(cot_ref[rows, :].astype(F32))

    chunks(block, body)
    down_grad_ref[...] += dot(cot_ref[...], top_ref[...], 0, 0)

    @pl.when(step == steps - 1)
    def _():
        part_out(place_ref, down_grad_ref, kept_ref, sent_ref)


def hand_out(place_ref, device, kept_ref, sent_ref, rows, part):
    m = (device // 2) ^ place_ref[0]

    @pl.when(place_ref[1] == device % 2)
    def _():
        kept_ref[m, rows, 0 : part.shape[1]] = part.astype(kept_ref.dtype)

    @pl.when(place_ref[1] != device % 2)
    def _():
        sent_ref[m, rows, 0 : part.shape[1]] = part.astype(sent_ref.dtype)


def part_out(place_ref, total_ref, kept_ref, sent_ref):
    share = kept_ref.shape[1]
    for device in range(2 * kept_ref.shape[0]):
        part = total_ref[device * share : (device + 1) * share, :]
        hand_out(place_ref, device, kept_ref, sent_ref, slice(None), part)


def conv_weight_kernel(
    low_ref, mid_ref, flags_ref, place_ref, kept_ref, sent_ref, padded_ref, total_ref, row_ref
):
    step, steps = pl.program_id(0), pl.num_programs(0)
    block, width = mid_ref.shape
    chips = kept_ref.shape[0]
    share = width // (2 * chips)

    @pl.when(step == 0)
    def _():
        fill_padded(padded_ref, low_ref)
        total_ref[...] = jnp.zeros_like(total_ref)

    mid = mid_ref[...].T
    for tap in range(KERNEL):
        other = shifted(padded_ref, flags_ref, step * block, block, KERNEL - 1 - tap)
        total_ref[tap] += dot(mid, other)

    @pl.when(step == steps - 1)
    def _():
        for device in range(2 * chips):
            for tap in range(KERNEL):
                row_ref[tap * share : (tap + 1) * share, :] = total_ref[tap, device * share : (device + 1) * share, :]
            hand_out(place_ref, device, kept_ref, sent_ref, slice(None), row_ref[...])


def mid_grad_kernel(
    low_ref, weight_ref, up_out_ref, act_ref, narrow_ref, flags_ref, place_ref,
    up_low_ref, sums_ref, kept_ref, sent_ref,
    padded_ref, grad_ref, total_ref,
):
    step, steps = pl.program_id(0), pl.num_programs(0)
    block, width = up_out_ref.shape

    @pl.when(step == 0)
    def _():
        fill_padded(padded_ref, low_ref)
        sums_ref[...] = jnp.zeros_like(sums_ref)
        total_ref[...] = jnp.zeros_like(total_ref)

    for tap in range(KERNEL):
        other = shifted(padded_ref, flags_ref, step * block, block, KERNEL - 1 - tap)
        term = dot(other, weight_ref[tap], 1, 1)
        grad_ref[...] = term if tap == 0 else grad_ref[...] + term
    gain, bias = narrow_ref[1:2, :], narrow_ref[2:3, :]

    def body(at):
        rows = pl.ds(at, ROWS)
        hat, scale = norm(up_out_ref[rows, :], width)
        slope = gelu_slope(hat * gain + bias) * flags_ref[rows, 0:1]
        back, by_gain, by_sum = norm_back(hat, scale, gain, slope, grad_ref[rows, :], width)
        up_low_ref[rows, :] = back.astype(BF16)
        sums_ref[0:8, :] += fold(by_gain)
        sums_ref[8:16, :] += fold(by_sum)
        sums_ref[16:24, :] += fold(back)

    chunks(block, body)
    total_ref[...] += dot(act_ref[...], up_low_ref[...], 0, 0)

    @pl.when(step == steps - 1)
    def _():
        part_out(place_ref, total_ref, kept_ref, sent_ref)


def input_grad_kernel(
    up_low_ref, weight_ref, x_ref, cot_ref, wide_ref, top_sums_ref, mid_sums_ref, cot_sums_ref, place_ref,
    out_ref, kept_ref, sent_ref,
    grad_ref, sums_ref, wide_row_ref, narrow_row_ref,
):
    step, steps = pl.program_id(0), pl.num_programs(0)
    block, width = out_ref.shape

    @pl.when(step == 0)
    def _():
        sums_ref[...] = jnp.zeros_like(sums_ref)

    grad_ref[...] = dot(up_low_ref[...], weight_ref[...], 1, 1)
    gain, bias = wide_ref[0:1, :], wide_ref[1:2, :]

    def body(at):
        rows = pl.ds(at, ROWS)
        hat, scale = norm(x_ref[rows, :].astype(F32), width)
        back, by_gain, by_sum = norm_back(hat, scale, gain, gelu_slope(hat * gain + bias), grad_ref[rows, :], width)
        out_ref[rows, :] = cot_ref[rows, :].astype(F32) + back
        sums_ref[0:8, :] += fold(by_gain)
        sums_ref[8:16, :] += fold(by_sum)

    chunks(block, body, unroll=2)

    @pl.when(step == steps - 1)
    def _():
        def row(ref, k):
            return jnp.sum(ref[8 * k : 8 * k + 8, :], axis=0, keepdims=True)

        wide_row_ref[...] = jnp.zeros_like(wide_row_ref)
        narrow_row_ref[...] = jnp.zeros_like(narrow_row_ref)
        for at, (ref, k) in enumerate(((sums_ref, 0), (sums_ref, 1), (cot_sums_ref, 0))):
            wide_row_ref[at : at + 1, :] = row(ref, k)
        rows = ((mid_sums_ref, 2), (mid_sums_ref, 0), (mid_sums_ref, 1), (top_sums_ref, 2), (top_sums_ref, 0), (top_sums_ref, 1))
        for at, (ref, k) in enumerate(rows):
            narrow_row_ref[at : at + 1, :] = row(ref, k)
        chips = kept_ref.shape[0]
        wide, narrow = width // (2 * chips), narrow_row_ref.shape[1] // (2 * chips)
        kept_ref[...] = jnp.zeros_like(kept_ref)
        sent_ref[...] = jnp.zeros_like(sent_ref)
        for device in range(2 * chips):
            wide_part = wide_row_ref[:, device * wide : (device + 1) * wide]
            narrow_part = narrow_row_ref[:, device * narrow : (device + 1) * narrow]
            hand_out(place_ref, device, kept_ref, sent_ref, slice(0, 8), wide_part)
            hand_out(place_ref, device, kept_ref, sent_ref, slice(8, 16), narrow_part)


def output_kernel(x_ref, top_ref, weight_ref, wide_ref, out_ref):
    product = dot(top_ref[...], weight_ref[...], 1, 1)
    out_ref[...] = (x_ref[...].astype(F32) + product + wide_ref[2:3, :]).astype(BF16)


def call(kernel, name, grid, ins, outs, scratch, flops, args):
    def spec(shape, rows):
        if rows == "smem":
            return pl.BlockSpec(memory_space=pltpu.SMEM)
        if rows is None:
            return pl.BlockSpec(shape, lambda i: (0,) * len(shape))
        return pl.BlockSpec((rows,) + tuple(shape[1:]), lambda i: (i,) + (0,) * (len(shape) - 1))

    moved = sum(a.size * a.dtype.itemsize for a in args) + sum(
        jax.ShapeDtypeStruct(*o[0]).size * jnp.dtype(o[0][1]).itemsize for o in outs
    )
    return pl.pallas_call(
        kernel,
        name=name,
        grid=(grid,),
        in_specs=[spec(a.shape, rows) for a, rows in zip(args, ins)],
        out_specs=[spec(o[0][0], o[1]) for o in outs],
        out_shape=[jax.ShapeDtypeStruct(*o[0]) for o in outs],
        scratch_shapes=scratch,
        compiler_params=pltpu.CompilerParams(vmem_limit_bytes=VMEM_BYTES),
        cost_estimate=pl.CostEstimate(flops=flops, bytes_accessed=moved, transcendentals=0),
    )(*args)


def flags_of(lengths_row, keep_mask):
    count = keep_mask.shape[0]
    ends = jnp.cumsum(lengths_row)
    position = jnp.arange(count, dtype=jnp.int32)[:, None]

    def segment(at):
        return jnp.sum((at >= ends[None, :]).astype(jnp.int32), axis=1, keepdims=True)

    own = segment(position)
    columns = [keep_mask[:, None] != 0]
    for tap in range(KERNEL):
        source = position + (tap - KERNEL // 2) * DILATION
        columns.append((source >= 0) & (source < count) & (segment(source) == own))
    columns += [columns[0]] * (8 - len(columns))
    return jnp.concatenate([column.astype(F32) for column in columns], axis=1)


def pack_small(wide, narrow):
    out = jnp.zeros((16, 128), BF16)
    for first, group in ((0, wide), (8, narrow)):
        for k, item in enumerate(group):
            out = out + jnp.pad(item[None, :], ((first + k, 15 - first - k), (0, 128 - item.shape[0])))
    return out


def body(
    axes,
    inputs,
    lengths,
    keep_mask,
    cotangent,
    ln1_gain,
    ln1_bias,
    up_weight,
    up_bias,
    ln2_gain,
    ln2_bias,
    conv_weight,
    conv_bias,
    ln3_gain,
    ln3_bias,
    down_weight,
    down_bias,
):
    count, model = inputs.shape
    inner = up_weight.shape[1]
    dp, columns = axes[0][1], axes[1][1]
    chips = dp * columns
    place = jnp.stack(
        [lax.axis_index("dp") * columns + lax.axis_index("chip"), lax.axis_index("core")]
    ).astype(jnp.int32)
    flags = flags_of(lengths[0], keep_mask)

    small = gather_all(
        pack_small(
            (ln1_gain, ln1_bias, down_bias),
            (up_bias, ln2_gain, ln2_bias, conv_bias, ln3_gain, ln3_bias),
        ),
        axes,
    )
    up_full = gather_all(up_weight, axes).reshape(model, inner)
    conv_pieces = gather_all(conv_weight.reshape(-1, inner), axes)
    down_full = gather_all(down_weight.T, axes).reshape(model, inner)

    full = functools.partial
    block = 256
    steps = count // block
    wide_up = 2 * count * model * inner
    wide_conv = 2 * count * KERNEL * inner * inner

    act_one, wide, narrow = call(
        first_act_kernel, "first_act", steps, (None, block),
        [(((count, model), BF16), block), (((8, model), F32), None), (((8, inner), F32), None)],
        [], 20 * count * model, (small, inputs),
    )
    up_out, mid = call(
        up_kernel, "up", steps, (block, None, None, block),
        [(((count, inner), F32), block), (((count, inner), BF16), block)],
        [], wide_up, (act_one, up_full, narrow, flags),
    )
    share, conv_share = model // (2 * chips), KERNEL * inner // (2 * chips)
    top, low, conv_full, top_sums, cot_sums, down_kept, down_sent = call(
        conv_kernel, "conv", steps, (None, None, None, block, None, block, "smem"),
        [
            (((count, inner), BF16), block),
            (((count, inner), BF16), block),
            (((KERNEL, inner, inner), BF16), None),
            (((24, inner), F32), None),
            (((8, model), F32), None),
            (((chips, share, inner), F32), None),
            (((chips, share, inner), BF16), None),
        ],
        [
            pltpu.VMEM((count + 2 * REACH, inner), F32),
            pltpu.VMEM((KERNEL, inner, inner), F32),
            pltpu.VMEM((conv_share, inner), F32),
            pltpu.VMEM((block, inner), F32),
            pltpu.VMEM((block, inner), F32),
            pltpu.VMEM((model, inner), F32),
        ],
        wide_conv + 2 * wide_up, (mid, conv_pieces, down_full, cotangent, narrow, flags, place),
    )
    down_own = scatter_all(
        down_kept.reshape(dp, columns, share, inner), down_sent.reshape(dp, columns, share, inner), axes, (1, 0)
    )
    conv_kept, conv_sent = call(
        conv_weight_kernel, "conv_weight", steps, (None, block, block, "smem"),
        [(((chips, conv_share, inner), F32), None), (((chips, conv_share, inner), BF16), None)],
        [
            pltpu.VMEM((count + 2 * REACH, inner), F32),
            pltpu.VMEM((KERNEL, inner, inner), F32),
            pltpu.VMEM((conv_share, inner), F32),
        ],
        wide_conv, (low, mid, flags, place),
    )
    conv_own = scatter_all(
        conv_kept.reshape(dp, columns, conv_share, inner), conv_sent.reshape(dp, columns, conv_share, inner), axes
    )
    up_low, mid_sums, up_kept, up_sent = call(
        mid_grad_kernel, "mid_grad", steps, (None, None, block, block, None, block, "smem"),
        [
            (((count, inner), BF16), block),
            (((24, inner), F32), None),
            (((chips, share, inner), F32), None),
            (((chips, share, inner), BF16), None),
        ],
        [
            pltpu.VMEM((count + 2 * REACH, inner), F32),
            pltpu.VMEM((block, inner), F32),
            pltpu.VMEM((model, inner), F32),
        ],
        wide_conv + wide_up, (low, conv_full, up_out, act_one, narrow, flags, place),
    )
    up_own = scatter_all(
        up_kept.reshape(dp, columns, share, inner), up_sent.reshape(dp, columns, share, inner), axes
    )
    input_grad, small_kept, small_sent = call(
        input_grad_kernel, "input_grad", steps,
        (block, None, block, block, None, None, None, None, "smem"),
        [
            (((count, model), F32), block),
            (((chips, 16, 128), F32), None),
            (((chips, 16, 128), F32), None),
        ],
        [
            pltpu.VMEM((block, model), F32),
            pltpu.VMEM((16, model), F32),
            pltpu.VMEM((8, model), F32),
            pltpu.VMEM((8, inner), F32),
        ],
        wide_up, (up_low, up_full, inputs, cotangent, wide, top_sums, mid_sums, cot_sums, place),
    )
    small_own = scatter_exact(
        small_kept.reshape(dp, columns, 16, 128), small_sent.reshape(dp, columns, 16, 128), axes
    )
    (output,) = call(
        output_kernel, "output", steps, (block, block, None, None),
        [(((count, model), BF16), block)],
        [], wide_up, (inputs, top, down_full, wide),
    )
    wide_row, narrow_row = up_weight.shape[0], conv_weight.shape[1]
    sums = [small_own[at, :wide_row] for at in range(2)]
    sums += [small_own[8 + at, :narrow_row] for at in range(6)]
    sums.append(small_own[2, :wide_row])
    return (output, input_grad, up_own, conv_own.reshape(conv_weight.shape), down_own.T) + tuple(sums)


def solution(mesh):
    rows, columns = mesh.shape["dp"], mesh.shape["fsdp"] // 2
    split = Mesh(mesh.devices.reshape(rows, columns, 2), ALL)
    axes = (("dp", rows), ("chip", columns), ("core", 2))
    by_row = P(ALL)
    by_second = P(None, ALL)
    in_specs = [by_row] * 16
    in_specs[10] = in_specs[14] = by_second
    out_specs = [by_row] * 14
    out_specs[3] = out_specs[4] = by_second
    return jax.shard_map(
        functools.partial(body, axes),
        mesh=split,
        in_specs=tuple(in_specs),
        out_specs=tuple(out_specs),
        check_vma=False,
    )
```

time: 709 us -> 374 us (0.53); the launches traced: 700 us -> 373 us
  waiting for transfers between devices: 336 us -> 75.3 us
  Pallas kernels: 0 us -> 192 us
  matrix products: 117 us -> 0 us
  local copies, waits for them, and re-layouts: 104 us -> 14.4 us
  blocking collectives: 82.3 us -> 0 us
  starting transfers between devices: 0.65 us -> 67.5 us
  other arithmetic: 45.5 us -> 22.5 us
  between operations: 15.2 us -> 1.29 us
    unnamed x9 -> x0, waiting for transfers between devices: 328 us -> none
    pallas_call x0 -> x7, Pallas kernels: none -> 192 us  [call(): pl.pallas_call(kernel, name=name, grid=(grid,), in_specs=[spec(a.shape, r...]
    dot_general x21 -> x0, matrix products: 117 us -> none  [the longest x7 43.3 us: last_dims(): lax.dot_general(left, right, (((1,), (1,)), ((), ())), preferred_element_...]
    unnamed x2 -> x0, blocking collectives: 82.3 us -> none
    ppermute x0 -> x56, waiting for transfers between devices: none -> 75.3 us  [swap(): return lax.ppermute(array, axis, [(k, k ^ mask) for k in range(size)])]
    ppermute x0 -> x56, starting transfers between devices: none -> 67.5 us  [swap(): return lax.ppermute(array, axis, [(k, k ^ mask) for k in range(size)])]
    gather x5 -> x0, local copies, waits for them, and re-layouts: 58.9 us -> none  [tap_masks(): matched = segment[jnp.clip(source, 0, count - 1)] == segment]
    reduce_sum x12 -> x1, other arithmetic: 32.1 us -> 0.17 us  [segment(): jnp.sum((at >= ends[None, :]).astype(jnp.int32), axis=1, keepdims=True)]
  transfers between devices with their start and end apart: 6 -> 56, of which waited for: 4 -> 17; matrix products, arithmetic and copies ran while one was open for 32% -> 7% of each run, Pallas kernels for 0% -> 16%
where the time goes in v2:
time: 374 us; the launch traced here: 373 us
  Pallas kernels  192 us (51%)
  waiting for transfers between devices  75.3 us (20%)
  starting transfers between devices  67.5 us (18%)
  other arithmetic  22.5 us (6%)
  local copies, waits for them, and re-layouts  14.4 us (4%)
    pallas_call x7, Pallas kernels, call(): pl.pallas_call(kernel, name=name, grid=(grid,), in_specs=[spec(a.shape, r...  192 us
    ppermute x56, waiting for transfers between devices, swap(): return lax.ppermute(array, axis, [(k, k ^ mask) for k in range(size)])  75.3 us
    ppermute x56, starting transfers between devices, swap(): return lax.ppermute(array, axis, [(k, k ^ mask) for k in range(size)])  67.5 us
    another operation x27, other arithmetic, gather_axis(): return jnp.stack(xor_order(held, lax.axis_index(axis)), place)  13.6 us
    another operation x6, local copies, waits for them, and re-layouts, gather_axis(): return jnp.stack(xor_order(held, lax.axis_index(axis)), place)  8.01 us
  transfers between devices with their start and end apart: 56, of which 17 were waited for; matrix products, arithmetic and copies ran while one was open for 7% of the time, Pallas kernels for 16%

profile of v2, /device:TPU:0, one launch (start us, length us, event | category | flops | bytes accessed | tf_op | source)
XLA Modules:
  0.0 372.7 jit_solution(14192588605739278747)
XLA Ops:
  1.5 3.1 collective-permute-start.2
  4.5 2.6 collective-permute-start.1
  8.0 3.5 collective-permute-start.22
  14.2 1.6 collective-permute-start.5
  15.8 1.5 collective-permute-start.4
  17.8 0.9 reshape.292
  20.3 1.6 collective-permute-done.3
  23.4 1.6 collective-permute-start.16
  25.3 1.6 collective-permute-start.15
  26.9 3.0 collective-permute-start.14
  30.9 1.5 collective-permute-start.12
  32.4 1.6 collective-permute-start.11
  34.0 2.7 collective-permute-done.15
  36.7 2.6 collective-permute-start.10
  40.3 1.4 collective-permute-start.19
  42.6 1.3 collective-permute-start.18
  43.8 1.8 collective-permute-done.10
  45.6 2.6 collective-permute-start.17
  48.4 1.0 pad_maximum_fusion.4
  49.4 11.9 %collective-permute-done.19 = bf16[4,100,640]{2,0,1:T(4,128)(2,1)S(1)} collective-permute-done((bf16[4,100,640]{2,0,1:T(4,128)(2,1)S(1)}, bf16[4,100,640]{2,0,1:T(4,128)(2,1)S(1)}, u32[]{:S(2)}, u32[]{:S(2)}) %collective-permute-start.19) | collective-permute-done | bytes 512032 | tf_op jit(solution)/shard_map/ppermute | solution.py:33
  61.5 2.6 collective-permute-start.24
  64.1 7.9 %collective-permute-done.17 = bf16[4,100,640]{2,0,1:T(4,128)(2,1)S(1)} collective-permute-done((bf16[4,100,640]{2,0,1:T(4,128)(2,1)S(1)}, bf16[4,100,640]{2,0,1:T(4,128)(2,1)S(1)}, u32[]{:S(2)}, u32[]{:S(2)}) %collective-permute-start.17) | collective-permute-done | bytes 512032 | tf_op jit(solution)/shard_map/ppermute | solution.py:33
  73.3 2.1 copy.103
  75.9 2.0 collective-permute-done.25
  78.7 1.1 pad_maximum_fusion.5
  80.5 1.1 copy.93
  81.5 2.0 concatenate.6.flags_ref
  85.1 12.6 %first_act.1 = (bf16[2048,1280]{1,0:T(8,128)(2,1)}, f32[8,1280]{1,0:T(8,128)}, f32[8,640]{1,0:T(8,128)}) custom-call(bf16[32,16,128]{2,1,0:T(8,128)(2,1)} %bitcast.254, bf16[2048,1280]{1,0:T(8,128)(2,1)} %x_ref.5), custom_call_target="tpu_custom_call" | custom-call | flops 52428800 | bytes 10678272 | tf_op jit(solution)/shard_map/first_act/pallas_call | solution.py:375
  97.7 1.4 select_bitcast_fusion.5
  99.3 1.3 copy.92
  100.6 1.4 select_bitcast_fusion.3
  102.2 1.3 copy.107
  103.5 17.1 %up.1 = (f32[2048,640]{1,0:T(8,128)}, bf16[2048,640]{1,0:T(8,128)(2,1)}) custom-call(bf16[2048,1280]{1,0:T(8,128)(2,1)} %get-tuple-element.35.act_ref, bf16[1280,640]{1,0:T(8,128)(2,1)} %bitcast.244, f32[8,640]{1,0:T(8,128)} %get-tuple-element.36.narrow_ref, f32[2048,8]{1,0:T(8,128)} %concatenate.6.flags_ref), custom_call_target="tpu_custom_call" | custom-call | flops 3355443200 | bytes 14831616 | tf_op jit(solution)/shard_map/up/pallas_call | solution.py:375
  120.6 3.5 select_bitcast_fusion.1
  124.6 2.4 copy.106
  127.0 47.2 %conv.1 = (bf16[2048,640]{1,0:T(8,128)(2,1)}, bf16[2048,640]{1,0:T(8,128)(2,1)}, bf16[5,640,640]{2,1,0:T(8,128)(2,1)}, f32[24,640]{1,0:T(8,128)}, f32[8,1280]{1,...) custom-call(bf16[2048,640]{1,0:T(8,128)(2,1)} %get-tuple-element.37.mid_ref, ...), custom_call_target="tpu_custom_call" | custom-call | flops 15099494400 | bytes 25583624 | tf_op jit(solution)/shard_map/conv/pallas_call | solution.py:375
  174.3 41.8 %mid_grad.1 = (bf16[2048,640]{1,0:T(8,128)(2,1)}, f32[24,640]{1,0:T(8,128)}, f32[16,40,640]{2,1,0:T(8,128)}, bf16[16,40,640]{2,1,0:T(8,128)(2,1)}) custom-call(bf16[2048,640]{1,0:T(8,128)(2,1)} %get-tuple-element.40.low_ref, bf16[5,640,640]{2,1,0:T(8,128)(2,1)} %get-tuple-element.41.weight_ref, f32[2048,640]{1,0:T(8,128)} %get-tuple-element.42.up_out_ref, ...), custom_call_target="tpu_custom_call" | custom-call | flops 11744051200 | bytes 22429704 | tf_op jit(solution)/shard_map/mid_grad/pallas_call | solution.py:375
  216.1 42.2 %input_grad.1 = (f32[2048,1280]{1,0:T(8,128)}, f32[16,16,128]{2,1,0:T(8,128)}, f32[16,16,128]{2,1,0:T(8,128)}) custom-call(bf16[2048,640]{1,0:T(8,128)(2,1)} %get-tuple-element.43.up_low_ref, bf16[1280,640]{1,0:T(8,128)(2,1)} %bitcast.245, bf16[2048,1280]{1,0:T(8,128)(2,1)} %x_ref.5, bf16[2048,1280]{1,0:T(8,128)(2,1)} %cot_ref.3, ...), custom_call_target="tpu_custom_call" | custom-call | flops 3355443200 | bytes 25698312 | tf_op jit(solution)/shard_map/input_grad/pallas_call | solution.py:375
  258.9 1.2 collective-permute-done.49
  260.0 0.9 add.259
  261.6 2.2 collective-permute-start.52
  264.6 19.9 %conv_weight.1 = (f32[16,100,640]{2,1,0:T(8,128)}, bf16[16,100,640]{2,1,0:T(8,128)(2,1)}) custom-call(bf16[2048,640]{1,0:T(8,128)(2,1)} %get-tuple-element.40.low_ref, bf16[2048,640]{1,0:T(8,128)(2,1)} %get-tuple-element.37.mid_ref, f32[2048,8]{1,0:T(8,128)} %concatenate.6.flags_ref, s32[2]{0:T(128)} %pad_add_fusion.1.place_ref), custom_call_target="tpu_custom_call" | custom-call | flops 8388608000 | bytes 11452424 | tf_op jit(solution)/shard_map/conv_weight/pallas_call | solution.py:375
  285.2 2.4 collective-permute-start.54
  287.6 1.3 collective-permute-start.55
  289.0 10.8 %output.1 = bf16[2048,1280]{1,0:T(8,128)(2,1)} custom-call(bf16[2048,1280]{1,0:T(8,128)(2,1)} %x_ref.5, bf16[2048,640]{1,0:T(8,128)(2,1)} %get-tuple-element.38.top_ref, bf16[1280,640]{1,0:T(8,128)(2,1)} %bitcast.243, f32[8,1280]{1,0:T(8,128)} %get-tuple-element.39.wide_ref), custom_call_target="tpu_custom_call" | custom-call | flops 3355443200 | bytes 14786560 | tf_op jit(solution)/shard_map/output/pallas_call | solution.py:375
  302.0 2.1 collective-permute-start.43
  304.1 2.5 collective-permute-start.45
  307.0 1.6 collective-permute-start.29
  308.5 1.3 collective-permute-done.43
  309.8 1.4 collective-permute-start.31
  311.3 5.7 %collective-permute-done.45 = bf16[4,40,640]{2,1,0:T(8,128)(2,1)S(1)} collective-permute-done((bf16[4,40,640]{2,1,0:T(8,128)(2,1)S(1)}, bf16[4,40,640]{2,1,0:T(8,128)(2,1)S(1)}, u32[]{:S(2)}, u32[]{:S(2)}) %collective-permute-start.45) | collective-permute-done | bytes 204832 | tf_op jit(solution)/shard_map/ppermute | solution.py:33
  317.5 6.7 %collective-permute-done.44 = bf16[4,40,640]{2,1,0:T(8,128)(2,1)S(1)} collective-permute-done((bf16[4,40,640]{2,1,0:T(8,128)(2,1)S(1)}, bf16[4,40,640]{2,1,0:T(8,128)(2,1)S(1)}, u32[]{:S(2)}, u32[]{:S(2)}) %collective-permute-start.44) | collective-permute-done | bytes 204832 | tf_op jit(solution)/shard_map/ppermute | solution.py:33
  324.4 1.5 collective-permute-start.46
  328.1 1.2 collective-permute-start.37
  329.3 1.4 collective-permute-start.38
  330.7 0.9 collective-permute-start.36
  331.8 1.2 collective-permute-start.47
  333.1 20.4 %collective-permute-done.47 = bf16[40,640]{1,0:T(8,128)(2,1)S(1)} collective-permute-done((bf16[40,640]{1,0:T(8,128)(2,1)S(1)}, bf16[40,640]{1,0:T(8,128)(2,1)S(1)}, u32[]{:S(2)}, u32[]{:S(2)}) %collective-permute-start.47) | collective-permute-done | bytes 51232 | tf_op jit(solution)/shard_map/ppermute | solution.py:33
  353.5 2.2 collective-permute-start.34
  356.6 2.2 collective-permute-start.39
  358.8 2.2 collective-permute-start.41
  361.1 2.5 collective-permute-done.33
  364.2 3.0 collective-permute-done.41
  367.2 4.7 %collective-permute-done.40 = bf16[100,640]{1,0:T(8,128)(2,1)S(1)} collective-permute-done((bf16[100,640]{1,0:T(8,128)(2,1)S(1)}, bf16[100,640]{1,0:T(8,128)(2,1)S(1)}, u32[]{:S(2)}, u32[]{:S(2)}) %collective-permute-start.40) | collective-permute-done | bytes 128032 | tf_op jit(solution)/shard_map/ppermute | solution.py:33
  (157 shorter events, 27.6 us)
Async XLA Ops:
  1.5 11.9 %collective-permute-start.2 = (bf16[16,128]{1,0:T(8,128)(2,1)S(1)}, bf16[16,128]{1,0:T(8,128)(2,1)S(1)}, u32[]{:S(2)}, u32[]{:S(2)}) collective-permute-start(bf16[16,128]{1,0:T(8,128)(2,1)S(1)} %pad_add_fusion), channel_id=1, source_target_pairs={{0,2},{2,0},{4,6},{6,4},{1,3},{3,1},{5,7},{7,5},{8,10},{10,8},{12,... | collective-permute-start | bytes 12296 | tf_op jit(solution)/shard_map/ppermute | solution.py:33
  4.5 8.8 %collective-permute-start.1 = (bf16[16,128]{1,0:T(8,128)(2,1)S(1)}, bf16[16,128]{1,0:T(8,128)(2,1)S(1)}, u32[]{:S(2)}, u32[]{:S(2)}) collective-permute-start(bf16[16,128]{1,0:T(8,128)(2,1)S(1)} %pad_add_fusion), channel_id=1, source_target_pairs={{0,4},{2,6},{4,0},{6,2},{1,5},{3,7},{5,1},{7,3},{8,12},{10,14},{12... | collective-permute-start | bytes 12296 | tf_op jit(solution)/shard_map/ppermute | solution.py:33
  7.1 6.2 %collective-permute-start = (bf16[16,128]{1,0:T(8,128)(2,1)S(1)}, bf16[16,128]{1,0:T(8,128)(2,1)S(1)}, u32[]{:S(2)}, u32[]{:S(2)}) collective-permute-start(bf16[16,128]{1,0:T(8,128)(2,1)S(1)} %pad_add_fusion), channel_id=1, source_target_pairs={{0,6},{2,4},{4,2},{6,0},{1,7},{3,5},{5,3},{7,1},{8,14},{10,12},{12... | collective-permute-start | bytes 12296 | tf_op jit(solution)/shard_map/ppermute | solution.py:33
  7.1 15.6 %collective-permute-start.23 = (bf16[40,640]{1,0:T(8,128)(2,1)}, bf16[40,640]{1,0:T(8,128)(2,1)S(1)}, u32[]{:S(2)}, u32[]{:S(2)}) collective-permute-start(bf16[40,640]{1,0:T(8,128)(2,1)} %bitcast.256), channel_id=1, source_target_pairs={{0,2},{2,0},{4,6},{6,4},{1,3},{3,1},{5,7},{7,5},{8,10},{10,8},{12,... | collective-permute-start | bytes 153608 | tf_op jit(solution)/shard_map/ppermute | solution.py:33
  8.0 15.3 %collective-permute-start.22 = (bf16[40,640]{1,0:T(8,128)(2,1)}, bf16[40,640]{1,0:T(8,128)(2,1)S(1)}, u32[]{:S(2)}, u32[]{:S(2)}) collective-permute-start(bf16[40,640]{1,0:T(8,128)(2,1)} %bitcast.257), channel_id=1, source_target_pairs={{0,4},{2,6},{4,0},{6,2},{1,5},{3,7},{5,1},{7,3},{8,12},{10,14},{12... | collective-permute-start | bytes 153608 | tf_op jit(solution)/shard_map/ppermute | solution.py:33
  14.2 4.5 %collective-permute-start.5 = (bf16[4,16,128]{2,1,0:T(8,128)(2,1)S(1)}, bf16[4,16,128]{2,1,0:T(8,128)(2,1)S(1)}, u32[]{:S(2)}, u32[]{:S(2)}) collective-permute-start(bf16[4,16,128]{2,1,0:T(8,128)(2,1)S(1)} %pad_maximum_fusion.11), channel_id=1, source_target_pairs={{0,8},{8,0},{16,24},{24,16},{1,9},{9,1},{17,25},{25,17},{2,10},{10... | collective-permute-start | bytes 49160 | tf_op jit(solution)/shard_map/ppermute | solution.py:33
  15.8 3.7 %collective-permute-start.4 = (bf16[4,16,128]{2,1,0:T(8,128)(2,1)S(1)}, bf16[4,16,128]{2,1,0:T(8,128)(2,1)S(1)}, u32[]{:S(2)}, u32[]{:S(2)}) collective-permute-start(bf16[4,16,128]{2,1,0:T(8,128)(2,1)S(1)} %pad_maximum_fusion.11), channel_id=1, source_target_pairs={{0,16},{8,24},{16,0},{24,8},{1,17},{9,25},{17,1},{25,9},{2,18},{10... | collective-permute-start | bytes 49160 | tf_op jit(solution)/shard_map/ppermute | solution.py:33
  17.3 4.6 %collective-permute-start.3 = (bf16[4,16,128]{2,1,0:T(8,128)(2,1)S(1)}, bf16[4,16,128]{2,1,0:T(8,128)(2,1)S(1)}, u32[]{:S(2)}, u32[]{:S(2)}) collective-permute-start(bf16[4,16,128]{2,1,0:T(8,128)(2,1)S(1)} %pad_maximum_fusion.11), channel_id=1, source_target_pairs={{0,24},{8,16},{16,8},{24,0},{1,25},{9,17},{17,9},{25,1},{2,26},{10... | collective-permute-start | bytes 49160 | tf_op jit(solution)/shard_map/ppermute | solution.py:33
  18.8 6.5 %collective-permute-start.21 = (bf16[40,640]{1,0:T(8,128)(2,1)}, bf16[40,640]{1,0:T(8,128)(2,1)S(1)}, u32[]{:S(2)}, u32[]{:S(2)}) collective-permute-start(bf16[40,640]{1,0:T(8,128)(2,1)} %bitcast.258), channel_id=1, source_target_pairs={{0,6},{2,4},{4,2},{6,0},{1,7},{3,5},{5,3},{7,1},{8,14},{10,12},{12... | collective-permute-start | bytes 153608 | tf_op jit(solution)/shard_map/ppermute | solution.py:33
  19.5 7.4 %collective-permute-start.8 = (bf16[40,640]{1,0:T(8,128)(2,1)}, bf16[40,640]{1,0:T(8,128)(2,1)S(1)}, u32[]{:S(2)}, u32[]{:S(2)}) collective-permute-start(bf16[40,640]{1,0:T(8,128)(2,1)} %param.22), channel_id=1, source_target_pairs={{0,4},{2,6},{4,0},{6,2},{1,5},{3,7},{5,1},{7,3},{8,12},{10,14},{12... | collective-permute-start | bytes 153608 | tf_op jit(solution)/shard_map/ppermute | solution.py:33
  21.9 8.0 %collective-permute-start.7 = (bf16[40,640]{1,0:T(8,128)(2,1)}, bf16[40,640]{1,0:T(8,128)(2,1)S(1)}, u32[]{:S(2)}, u32[]{:S(2)}) collective-permute-start(bf16[40,640]{1,0:T(8,128)(2,1)} %param.22), channel_id=1, source_target_pairs={{0,6},{2,4},{4,2},{6,0},{1,7},{3,5},{5,3},{7,1},{8,14},{10,12},{12... | collective-permute-start | bytes 153608 | tf_op jit(solution)/shard_map/ppermute | solution.py:33
  22.8 7.2 %collective-permute-start.9 = (bf16[40,640]{1,0:T(8,128)(2,1)}, bf16[40,640]{1,0:T(8,128)(2,1)S(1)}, u32[]{:S(2)}, u32[]{:S(2)}) collective-permute-start(bf16[40,640]{1,0:T(8,128)(2,1)} %param.22), channel_id=1, source_target_pairs={{0,2},{2,0},{4,6},{6,4},{1,3},{3,1},{5,7},{7,5},{8,10},{10,8},{12,... | collective-permute-start | bytes 153608 | tf_op jit(solution)/shard_map/ppermute | solution.py:33
  23.4 9.1 %collective-permute-start.16 = (bf16[100,640]{1,0:T(8,128)(2,1)S(1)}, bf16[100,640]{1,0:T(8,128)(2,1)S(1)}, u32[]{:S(2)}, u32[]{:S(2)}) collective-permute-start(bf16[100,640]{1,0:T(8,128)(2,1)S(1)} %reshape.292), channel_id=1, source_target_pairs={{0,2},{2,0},{4,6},{6,4},{1,3},{3,1},{5,7},{7,5},{8,10},{10,8},{12,... | collective-permute-start | bytes 384008 | tf_op jit(solution)/shard_map/ppermute | solution.py:33
  25.3 11.4 %collective-permute-start.15 = (bf16[100,640]{1,0:T(8,128)(2,1)S(1)}, bf16[100,640]{1,0:T(8,128)(2,1)S(1)}, u32[]{:S(2)}, u32[]{:S(2)}) collective-permute-start(bf16[100,640]{1,0:T(8,128)(2,1)S(1)} %reshape.292), channel_id=1, source_target_pairs={{0,4},{2,6},{4,0},{6,2},{1,5},{3,7},{5,1},{7,3},{8,12},{10,14},{12... | collective-permute-start | bytes 384008 | tf_op jit(solution)/shard_map/ppermute | solution.py:33
  26.9 12.3 %collective-permute-start.14 = (bf16[100,640]{1,0:T(8,128)(2,1)S(1)}, bf16[100,640]{1,0:T(8,128)(2,1)S(1)}, u32[]{:S(2)}, u32[]{:S(2)}) collective-permute-start(bf16[100,640]{1,0:T(8,128)(2,1)S(1)} %reshape.292), channel_id=1, source_target_pairs={{0,6},{2,4},{4,2},{6,0},{1,7},{3,5},{5,3},{7,1},{8,14},{10,12},{12... | collective-permute-start | bytes 384008 | tf_op jit(solution)/shard_map/ppermute | solution.py:33
  30.0 53.6 %collective-permute-start.6 = (bf16[4,4,16,128]{3,2,1,0:T(8,128)(2,1)S(1)}, bf16[4,4,16,128]{3,2,1,0:T(8,128)(2,1)}, u32[]{:S(2)}, u32[]{:S(2)}) collective-permute-start(bf16[4,4,16,128]{3,2,1,0:T(8,128)(2,1)S(1)} %pad_maximum_fusion.10), channel_id=1, source_target_pairs={{0,1},{1,0},{2,3},{3,2},{4,5},{5,4},{6,7},{7,6},{8,9},{9,8},{10,11... | collective-permute-start | bytes 196616 | tf_op jit(solution)/shard_map/ppermute | solution.py:33
  30.9 9.4 %collective-permute-start.12 = (bf16[4,40,640]{2,1,0:T(8,128)(2,1)S(1)}, bf16[4,40,640]{2,1,0:T(8,128)(2,1)S(1)}, u32[]{:S(2)}, u32[]{:S(2)}) collective-permute-start(bf16[4,40,640]{2,1,0:T(8,128)(2,1)S(1)} %pad_maximum_fusion.7), channel_id=1, source_target_pairs={{0,8},{8,0},{16,24},{24,16},{1,9},{9,1},{17,25},{25,17},{2,10},{10... | collective-permute-start | bytes 614408 | tf_op jit(solution)/shard_map/ppermute | solution.py:33
  32.4 10.1 %collective-permute-start.11 = (bf16[4,40,640]{2,1,0:T(8,128)(2,1)S(1)}, bf16[4,40,640]{2,1,0:T(8,128)(2,1)S(1)}, u32[]{:S(2)}, u32[]{:S(2)}) collective-permute-start(bf16[4,40,640]{2,1,0:T(8,128)(2,1)S(1)} %pad_maximum_fusion.7), channel_id=1, source_target_pairs={{0,16},{8,24},{16,0},{24,8},{1,17},{9,25},{17,1},{25,9},{2,18},{10... | collective-permute-start | bytes 614408 | tf_op jit(solution)/shard_map/ppermute | solution.py:33
  36.7 8.9 %collective-permute-start.10 = (bf16[4,40,640]{2,1,0:T(8,128)(2,1)S(1)}, bf16[4,40,640]{2,1,0:T(8,128)(2,1)S(1)}, u32[]{:S(2)}, u32[]{:S(2)}) collective-permute-start(bf16[4,40,640]{2,1,0:T(8,128)(2,1)S(1)} %pad_maximum_fusion.7), channel_id=1, source_target_pairs={{0,24},{8,16},{16,8},{24,0},{1,25},{9,17},{17,9},{25,1},{2,26},{10... | collective-permute-start | bytes 614408 | tf_op jit(solution)/shard_map/ppermute | solution.py:33
  39.3 36.1 %collective-permute-start.26 = (bf16[4,40,640]{2,1,0:T(8,128)(2,1)S(1)}, bf16[4,40,640]{2,1,0:T(8,128)(2,1)S(1)}, u32[]{:S(2)}, u32[]{:S(2)}) collective-permute-start(bf16[4,40,640]{2,1,0:T(8,128)(2,1)S(1)} %pad_maximum_fusion.8), channel_id=1, source_target_pairs={{0,8},{8,0},{16,24},{24,16},{1,9},{9,1},{17,25},{25,17},{2,10},{10... | collective-permute-start | bytes 614408 | tf_op jit(solution)/shard_map/ppermute | solution.py:33
  40.3 21.0 %collective-permute-start.19 = (bf16[4,100,640]{2,0,1:T(4,128)(2,1)S(1)}, bf16[4,100,640]{2,0,1:T(4,128)(2,1)S(1)}, u32[]{:S(2)}, u32[]{:S(2)}) collective-permute-start(bf16[4,100,640]{2,0,1:T(4,128)(2,1)S(1)} %copy.94), channel_id=1, source_target_pairs={{0,8},{8,0},{16,24},{24,16},{1,9},{9,1},{17,25},{25,17},{2,10},{10... | collective-permute-start | bytes 1536008 | tf_op jit(solution)/shard_map/ppermute | solution.py:33
  42.6 18.9 %collective-permute-start.18 = (bf16[4,100,640]{2,0,1:T(4,128)(2,1)S(1)}, bf16[4,100,640]{2,0,1:T(4,128)(2,1)S(1)}, u32[]{:S(2)}, u32[]{:S(2)}) collective-permute-start(bf16[4,100,640]{2,0,1:T(4,128)(2,1)S(1)} %copy.94), channel_id=1, source_target_pairs={{0,16},{8,24},{16,0},{24,8},{1,17},{9,25},{17,1},{25,9},{2,18},{10... | collective-permute-start | bytes 1536008 | tf_op jit(solution)/shard_map/ppermute | solution.py:33
  45.6 26.4 %collective-permute-start.17 = (bf16[4,100,640]{2,0,1:T(4,128)(2,1)S(1)}, bf16[4,100,640]{2,0,1:T(4,128)(2,1)S(1)}, u32[]{:S(2)}, u32[]{:S(2)}) collective-permute-start(bf16[4,100,640]{2,0,1:T(4,128)(2,1)S(1)} %copy.94), channel_id=1, source_target_pairs={{0,24},{8,16},{16,8},{24,0},{1,25},{9,17},{17,9},{25,1},{2,26},{10... | collective-permute-start | bytes 1536008 | tf_op jit(solution)/shard_map/ppermute | solution.py:33
  48.2 23.8 %copy-start.1 = (bf16[1,4,40,640]{3,2,1,0:T(8,128)(2,1)}, bf16[1,4,40,640]{3,2,1,0:T(8,128)(2,1)S(1)}, u32[]{:S(2)}) copy-start(bf16[1,4,40,640]{3,2,1,0:T(8,128)(2,1)S(1)} %select_bitcast_fusion.14) | copy-start | bytes 614404
  61.3 16.5 %collective-permute-start.25 = (bf16[4,40,640]{2,1,0:T(8,128)(2,1)S(1)}, bf16[4,40,640]{2,1,0:T(8,128)(2,1)S(1)}, u32[]{:S(2)}, u32[]{:S(2)}) collective-permute-start(bf16[4,40,640]{2,1,0:T(8,128)(2,1)S(1)} %pad_maximum_fusion.8), channel_id=1, source_target_pairs={{0,16},{8,24},{16,0},{24,8},{1,17},{9,25},{17,1},{25,9},{2,18},{10... | collective-permute-start | bytes 614408 | tf_op jit(solution)/shard_map/ppermute | solution.py:33
  61.5 16.3 %collective-permute-start.24 = (bf16[4,40,640]{2,1,0:T(8,128)(2,1)S(1)}, bf16[4,40,640]{2,1,0:T(8,128)(2,1)S(1)}, u32[]{:S(2)}, u32[]{:S(2)}) collective-permute-start(bf16[4,40,640]{2,1,0:T(8,128)(2,1)S(1)} %pad_maximum_fusion.8), channel_id=1, source_target_pairs={{0,24},{8,16},{16,8},{24,0},{1,25},{9,17},{17,9},{25,1},{2,26},{10... | collective-permute-start | bytes 614408 | tf_op jit(solution)/shard_map/ppermute | solution.py:33
  72.0 25.6 %collective-permute-start.13 = (bf16[4,4,40,640]{3,2,1,0:T(8,128)(2,1)}, bf16[4,4,40,640]{3,2,1,0:T(8,128)(2,1)}, u32[]{:S(2)}, u32[]{:S(2)}) collective-permute-start(bf16[4,4,40,640]{3,2,1,0:T(8,128)(2,1)} %pad_maximum_fusion.4), channel_id=1, source_target_pairs={{0,1},{1,0},{2,3},{3,2},{4,5},{5,4},{6,7},{7,6},{8,9},{9,8},{10,11... | collective-permute-start | bytes 2457608 | tf_op jit(solution)/shard_map/ppermute | solution.py:33
  75.4 45.2 %collective-permute-start.20 = (bf16[4,4,100,640]{3,1,2,0:T(4,128)(2,1)}, bf16[4,4,100,640]{3,1,2,0:T(4,128)(2,1)}, u32[]{:S(2)}, u32[]{:S(2)}) collective-permute-start(bf16[4,4,100,640]{3,1,2,0:T(4,128)(2,1)} %copy.103), channel_id=1, source_target_pairs={{0,1},{1,0},{2,3},{3,2},{4,5},{5,4},{6,7},{7,6},{8,9},{9,8},{10,11... | collective-permute-start | bytes 6144008 | tf_op jit(solution)/shard_map/ppermute | solution.py:33
  79.8 20.8 %collective-permute-start.27 = (bf16[4,4,40,640]{3,2,1,0:T(8,128)(2,1)}, bf16[4,4,40,640]{3,2,1,0:T(8,128)(2,1)}, u32[]{:S(2)}, u32[]{:S(2)}) collective-permute-start(bf16[4,4,40,640]{3,2,1,0:T(8,128)(2,1)} %pad_maximum_fusion.5), channel_id=1, source_target_pairs={{0,1},{1,0},{2,3},{3,2},{4,5},{5,4},{6,7},{7,6},{8,9},{9,8},{10,11... | collective-permute-start | bytes 2457608 | tf_op jit(solution)/shard_map/ppermute | solution.py:33
  85.1 12.6 %copy-start.2 = (bf16[1,4,40,640]{3,2,1,0:T(8,128)(2,1)S(1)}, bf16[1,4,40,640]{3,2,1,0:T(8,128)(2,1)}, u32[]{:S(2)}) copy-start(bf16[1,4,40,640]{3,2,1,0:T(8,128)(2,1)} %copy-done.1) | copy-start | bytes 614404
  258.3 1.8 collective-permute-start.49
  261.0 24.2 %collective-permute-start.51 = (f32[4,16,128]{2,1,0:T(8,128)S(1)}, f32[4,16,128]{2,1,0:T(8,128)S(1)}, u32[]{:S(2)}, u32[]{:S(2)}) collective-permute-start(f32[4,16,128]{2,1,0:T(8,128)S(1)} %get-tuple-element.118), channel_id=1, source_target_pairs={{0,16},{8,24},{16,0},{24,8},{1,17},{9,25},{17,1},{25,9},{2,18},{10... | collective-permute-start | bytes 98312 | tf_op jit(solution)/shard_map/ppermute | solution.py:33
  261.6 23.6 %collective-permute-start.52 = (f32[4,16,128]{2,1,0:T(8,128)S(1)}, f32[4,16,128]{2,1,0:T(8,128)S(1)}, u32[]{:S(2)}, u32[]{:S(2)}) collective-permute-start(f32[4,16,128]{2,1,0:T(8,128)S(1)} %get-tuple-element.119), channel_id=1, source_target_pairs={{0,24},{8,16},{16,8},{24,0},{1,25},{9,17},{17,9},{25,1},{2,26},{10... | collective-permute-start | bytes 98312 | tf_op jit(solution)/shard_map/ppermute | solution.py:33
  263.8 20.7 %copy-start.7 = (bf16[16,40,640]{2,1,0:T(8,128)(2,1)S(1)}, bf16[16,40,640]{2,1,0:T(8,128)(2,1)}, u32[]{:S(2)}) copy-start(bf16[16,40,640]{2,1,0:T(8,128)(2,1)} %get-tuple-element.53) | copy-start | bytes 2457604
  263.8 20.8 %copy-start.8 = (bf16[16,40,640]{2,1,0:T(8,128)(2,1)S(1)}, bf16[16,40,640]{2,1,0:T(8,128)(2,1)}, u32[]{:S(2)}) copy-start(bf16[16,40,640]{2,1,0:T(8,128)(2,1)} %get-tuple-element.49) | copy-start | bytes 2457604
  263.8 21.4 %collective-permute-start.50 = (f32[4,16,128]{2,1,0:T(8,128)S(1)}, f32[4,16,128]{2,1,0:T(8,128)S(1)}, u32[]{:S(2)}, u32[]{:S(2)}) collective-permute-start(f32[4,16,128]{2,1,0:T(8,128)S(1)} %get-tuple-element.120), channel_id=1, source_target_pairs={{0,8},{8,0},{16,24},{24,16},{1,9},{9,1},{17,25},{25,17},{2,10},{10... | collective-permute-start | bytes 98312 | tf_op jit(solution)/shard_map/ppermute | solution.py:33
  284.6 17.2 %collective-permute-start.42 = (bf16[4,4,40,640]{3,2,0,1:T(8,128)(2,1)S(1)}, bf16[4,4,40,640]{3,2,0,1:T(8,128)(2,1)S(1)}, u32[]{:S(2)}, u32[]{:S(2)}) collective-permute-start(bf16[4,4,40,640]{3,2,0,1:T(8,128)(2,1)S(1)} %copy.116), channel_id=1, source_target_pairs={{0,1},{1,0},{2,3},{3,2},{4,5},{5,4},{6,7},{7,6},{8,9},{9,8},{10,11... | collective-permute-start | bytes 2457608 | tf_op jit(solution)/shard_map/ppermute | solution.py:33
  284.7 21.9 %collective-permute-start.28 = (bf16[4,4,40,640]{3,2,1,0:T(8,128)(2,1)S(1)}, bf16[4,4,40,640]{3,2,1,0:T(8,128)(2,1)S(1)}, u32[]{:S(2)}, u32[]{:S(2)}) collective-permute-start(bf16[4,4,40,640]{3,2,1,0:T(8,128)(2,1)S(1)} %bitcast.278), channel_id=1, source_target_pairs={{0,1},{1,0},{2,3},{3,2},{4,5},{5,4},{6,7},{7,6},{8,9},{9,8},{10,11... | collective-permute-start | bytes 2457608 | tf_op jit(solution)/shard_map/ppermute | solution.py:33
  285.2 15.4 %collective-permute-start.54 = (f32[16,128]{1,0:T(8,128)S(1)}, f32[16,128]{1,0:T(8,128)S(1)}, u32[]{:S(2)}, u32[]{:S(2)}) collective-permute-start(f32[16,128]{1,0:T(8,128)S(1)} %get-tuple-element.126), channel_id=1, source_target_pairs={{0,4},{2,6},{4,0},{6,2},{1,5},{3,7},{5,1},{7,3},{8,12},{10,14},{12... | collective-permute-start | bytes 24584 | tf_op jit(solution)/shard_map/ppermute | solution.py:33
  287.6 13.0 %collective-permute-start.55 = (f32[16,128]{1,0:T(8,128)S(1)}, f32[16,128]{1,0:T(8,128)S(1)}, u32[]{:S(2)}, u32[]{:S(2)}) collective-permute-start(f32[16,128]{1,0:T(8,128)S(1)} %get-tuple-element.127), channel_id=1, source_target_pairs={{0,6},{2,4},{4,2},{6,0},{1,7},{3,5},{5,3},{7,1},{8,14},{10,12},{12... | collective-permute-start | bytes 24584 | tf_op jit(solution)/shard_map/ppermute | solution.py:33
  289.0 11.7 %collective-permute-start.53 = (f32[16,128]{1,0:T(8,128)S(1)}, f32[16,128]{1,0:T(8,128)S(1)}, u32[]{:S(2)}, u32[]{:S(2)}) collective-permute-start(f32[16,128]{1,0:T(8,128)S(1)} %get-tuple-element.128), channel_id=1, source_target_pairs={{0,2},{2,0},{4,6},{6,4},{1,3},{3,1},{5,7},{7,5},{8,10},{10,8},{12,... | collective-permute-start | bytes 24584 | tf_op jit(solution)/shard_map/ppermute | solution.py:33
  289.0 10.8 %copy-start = (bf16[16,100,640]{2,1,0:T(8,128)(2,1)S(1)}, bf16[16,100,640]{2,1,0:T(8,128)(2,1)}, u32[]{:S(2)}) copy-start(bf16[16,100,640]{2,1,0:T(8,128)(2,1)} %get-tuple-element.51) | copy-start | bytes 6144004
  300.6 25.3 %collective-permute-start.35 = (bf16[4,4,100,640]{3,1,2,0:T(4,128)(2,1)S(1)}, bf16[4,4,100,640]{3,1,2,0:T(4,128)(2,1)S(1)}, u32[]{:S(2)}, u32[]{:S(2)}) collective-permute-start(bf16[4,4,100,640]{3,1,2,0:T(4,128)(2,1)S(1)} %copy.108), channel_id=1, source_target_pairs={{0,1},{1,0},{2,3},{3,2},{4,5},{5,4},{6,7},{7,6},{8,9},{9,8},{10,11... | collective-permute-start | bytes 6144008 | tf_op jit(solution)/shard_map/ppermute | solution.py:33
  301.8 4.9 %copy-start.5 = (f32[16,40,640]{2,1,0:T(8,128)S(1)}, f32[16,40,640]{2,1,0:T(8,128)}, u32[]{:S(2)}) copy-start(f32[16,40,640]{2,1,0:T(8,128)} %get-tuple-element.48) | copy-start | bytes 4915204
  302.0 7.8 %collective-permute-start.43 = (bf16[4,40,640]{2,1,0:T(8,128)(2,1)S(1)}, bf16[4,40,640]{2,1,0:T(8,128)(2,1)S(1)}, u32[]{:S(2)}, u32[]{:S(2)}) collective-permute-start(bf16[4,40,640]{2,1,0:T(8,128)(2,1)S(1)} %get-tuple-element.85), channel_id=1, source_target_pairs={{0,2},{2,0},{4,6},{6,4},{1,3},{3,1},{5,7},{7,5},{8,10},{10,8},{12,... | collective-permute-start | bytes 614408 | tf_op jit(solution)/shard_map/ppermute | solution.py:33
  304.1 12.8 %collective-permute-start.45 = (bf16[4,40,640]{2,1,0:T(8,128)(2,1)S(1)}, bf16[4,40,640]{2,1,0:T(8,128)(2,1)S(1)}, u32[]{:S(2)}, u32[]{:S(2)}) collective-permute-start(bf16[4,40,640]{2,1,0:T(8,128)(2,1)S(1)} %get-tuple-element.86), channel_id=1, source_target_pairs={{0,6},{2,4},{4,2},{6,0},{1,7},{3,5},{5,3},{7,1},{8,14},{10,12},{12... | collective-permute-start | bytes 614408 | tf_op jit(solution)/shard_map/ppermute | solution.py:33
  306.6 17.6 %collective-permute-start.44 = (bf16[4,40,640]{2,1,0:T(8,128)(2,1)S(1)}, bf16[4,40,640]{2,1,0:T(8,128)(2,1)S(1)}, u32[]{:S(2)}, u32[]{:S(2)}) collective-permute-start(bf16[4,40,640]{2,1,0:T(8,128)(2,1)S(1)} %get-tuple-element.87), channel_id=1, source_target_pairs={{0,4},{2,6},{4,0},{6,2},{1,5},{3,7},{5,1},{7,3},{8,12},{10,14},{12... | collective-permute-start | bytes 614408 | tf_op jit(solution)/shard_map/ppermute | solution.py:33
  306.6 20.2 %slice-start = ((s8[4259840]{0:T(1024)(128)(4,1)}), s8[4194304]{0:T(1024)(128)(4,1)S(1)}, s32[]{:S(2)}) async-start(s8[4259840]{0:T(1024)(128)(4,1)} %bitcast.246), calls=%async_computation | async-start | bytes 8388608
  306.6 20.2 %slice-start.1 = ((s8[4259840]{0:T(1024)(128)(4,1)}), s8[65536]{0:T(1024)(128)(4,1)S(1)}, s32[]{:S(2)}) async-start(s8[4259840]{0:T(1024)(128)(4,1)} %bitcast.246), calls=%async_computation.1 | async-start | bytes 131072
  307.0 21.1 %collective-permute-start.29 = (bf16[4,40,640]{2,1,0:T(8,128)(2,1)S(1)}, bf16[4,40,640]{2,1,0:T(8,128)(2,1)S(1)}, u32[]{:S(2)}, u32[]{:S(2)}) collective-permute-start(bf16[4,40,640]{2,1,0:T(8,128)(2,1)S(1)} %get-tuple-element.88), channel_id=1, source_target_pairs={{0,8},{8,0},{16,24},{24,16},{1,9},{9,1},{17,25},{25,17},{2,10},{10... | collective-permute-start | bytes 614408 | tf_op jit(solution)/shard_map/ppermute | solution.py:33
  309.8 19.5 %collective-permute-start.31 = (bf16[4,40,640]{2,1,0:T(8,128)(2,1)S(1)}, bf16[4,40,640]{2,1,0:T(8,128)(2,1)S(1)}, u32[]{:S(2)}, u32[]{:S(2)}) collective-permute-start(bf16[4,40,640]{2,1,0:T(8,128)(2,1)S(1)} %get-tuple-element.89), channel_id=1, source_target_pairs={{0,24},{8,16},{16,8},{24,0},{1,25},{9,17},{17,9},{25,1},{2,26},{10... | collective-permute-start | bytes 614408 | tf_op jit(solution)/shard_map/ppermute | solution.py:33
  317.0 13.8 %collective-permute-start.30 = (bf16[4,40,640]{2,1,0:T(8,128)(2,1)S(1)}, bf16[4,40,640]{2,1,0:T(8,128)(2,1)S(1)}, u32[]{:S(2)}, u32[]{:S(2)}) collective-permute-start(bf16[4,40,640]{2,1,0:T(8,128)(2,1)S(1)} %get-tuple-element.90), channel_id=1, source_target_pairs={{0,16},{8,24},{16,0},{24,8},{1,17},{9,25},{17,1},{25,9},{2,18},{10... | collective-permute-start | bytes 614408 | tf_op jit(solution)/shard_map/ppermute | solution.py:33
  324.4 7.4 %collective-permute-start.46 = (bf16[40,640]{1,0:T(8,128)(2,1)S(1)}, bf16[40,640]{1,0:T(8,128)(2,1)S(1)}, u32[]{:S(2)}, u32[]{:S(2)}) collective-permute-start(bf16[40,640]{1,0:T(8,128)(2,1)S(1)} %get-tuple-element.104), channel_id=1, source_target_pairs={{0,8},{8,0},{16,24},{24,16},{1,9},{9,1},{17,25},{25,17},{2,10},{10... | collective-permute-start | bytes 153608 | tf_op jit(solution)/shard_map/ppermute | solution.py:33
  325.9 7.1 %collective-permute-start.48 = (bf16[40,640]{1,0:T(8,128)(2,1)S(1)}, bf16[40,640]{1,0:T(8,128)(2,1)S(1)}, u32[]{:S(2)}, u32[]{:S(2)}) collective-permute-start(bf16[40,640]{1,0:T(8,128)(2,1)S(1)} %get-tuple-element.105), channel_id=1, source_target_pairs={{0,24},{8,16},{16,8},{24,0},{1,25},{9,17},{17,9},{25,1},{2,26},{10... | collective-permute-start | bytes 153608 | tf_op jit(solution)/shard_map/ppermute | solution.py:33
  328.1 28.3 %collective-permute-start.37 = (bf16[4,100,640]{2,0,1:T(4,128)(2,1)S(1)}, bf16[4,100,640]{2,0,1:T(4,128)(2,1)S(1)}, u32[]{:S(2)}, u32[]{:S(2)}) collective-permute-start(bf16[4,100,640]{2,0,1:T(4,128)(2,1)S(1)} %copy.112), channel_id=1, source_target_pairs={{0,16},{8,24},{16,0},{24,8},{1,17},{9,25},{17,1},{25,9},{2,18},{10... | collective-permute-start | bytes 1536008 | tf_op jit(solution)/shard_map/ppermute | solution.py:33
  329.3 27.0 %collective-permute-start.38 = (bf16[4,100,640]{2,0,1:T(4,128)(2,1)S(1)}, bf16[4,100,640]{2,0,1:T(4,128)(2,1)S(1)}, u32[]{:S(2)}, u32[]{:S(2)}) collective-permute-start(bf16[4,100,640]{2,0,1:T(4,128)(2,1)S(1)} %copy.114), channel_id=1, source_target_pairs={{0,24},{8,16},{16,8},{24,0},{1,25},{9,17},{17,9},{25,1},{2,26},{10... | collective-permute-start | bytes 1536008 | tf_op jit(solution)/shard_map/ppermute | solution.py:33
  330.7 25.6 %collective-permute-start.36 = (bf16[4,100,640]{2,0,1:T(4,128)(2,1)S(1)}, bf16[4,100,640]{2,0,1:T(4,128)(2,1)S(1)}, u32[]{:S(2)}, u32[]{:S(2)}) collective-permute-start(bf16[4,100,640]{2,0,1:T(4,128)(2,1)S(1)} %copy.110), channel_id=1, source_target_pairs={{0,8},{8,0},{16,24},{24,16},{1,9},{9,1},{17,25},{25,17},{2,10},{10... | collective-permute-start | bytes 1536008 | tf_op jit(solution)/shard_map/ppermute | solution.py:33
  331.8 21.7 %collective-permute-start.47 = (bf16[40,640]{1,0:T(8,128)(2,1)S(1)}, bf16[40,640]{1,0:T(8,128)(2,1)S(1)}, u32[]{:S(2)}, u32[]{:S(2)}) collective-permute-start(bf16[40,640]{1,0:T(8,128)(2,1)S(1)} %get-tuple-element.106), channel_id=1, source_target_pairs={{0,16},{8,24},{16,0},{24,8},{1,17},{9,25},{17,1},{25,9},{2,18},{10... | collective-permute-start | bytes 153608 | tf_op jit(solution)/shard_map/ppermute | solution.py:33
  333.0 28.0 %collective-permute-start.32 = (bf16[40,640]{1,0:T(8,128)(2,1)S(1)}, bf16[40,640]{1,0:T(8,128)(2,1)S(1)}, u32[]{:S(2)}, u32[]{:S(2)}) collective-permute-start(bf16[40,640]{1,0:T(8,128)(2,1)S(1)} %get-tuple-element.107), channel_id=1, source_target_pairs={{0,2},{2,0},{4,6},{6,4},{1,3},{3,1},{5,7},{7,5},{8,10},{10,8},{12,... | collective-permute-start | bytes 153608 | tf_op jit(solution)/shard_map/ppermute | solution.py:33
  353.5 7.6 %collective-permute-start.34 = (bf16[40,640]{1,0:T(8,128)(2,1)S(1)}, bf16[40,640]{1,0:T(8,128)(2,1)S(1)}, u32[]{:S(2)}, u32[]{:S(2)}) collective-permute-start(bf16[40,640]{1,0:T(8,128)(2,1)S(1)} %get-tuple-element.108), channel_id=1, source_target_pairs={{0,6},{2,4},{4,2},{6,0},{1,7},{3,5},{5,3},{7,1},{8,14},{10,12},{12... | collective-permute-start | bytes 153608 | tf_op jit(solution)/shard_map/ppermute | solution.py:33
  356.3 7.2 %collective-permute-start.33 = (bf16[40,640]{1,0:T(8,128)(2,1)S(1)}, bf16[40,640]{1,0:T(8,128)(2,1)S(1)}, u32[]{:S(2)}, u32[]{:S(2)}) collective-permute-start(bf16[40,640]{1,0:T(8,128)(2,1)S(1)} %get-tuple-element.109), channel_id=1, source_target_pairs={{0,4},{2,6},{4,0},{6,2},{1,5},{3,7},{5,1},{7,3},{8,12},{10,14},{12... | collective-permute-start | bytes 153608 | tf_op jit(solution)/shard_map/ppermute | solution.py:33
  356.6 7.6 %collective-permute-start.39 = (bf16[100,640]{1,0:T(8,128)(2,1)S(1)}, bf16[100,640]{1,0:T(8,128)(2,1)S(1)}, u32[]{:S(2)}, u32[]{:S(2)}) collective-permute-start(bf16[100,640]{1,0:T(8,128)(2,1)S(1)} %get-tuple-element.97), channel_id=1, source_target_pairs={{0,2},{2,0},{4,6},{6,4},{1,3},{3,1},{5,7},{7,5},{8,10},{10,8},{12,... | collective-permute-start | bytes 384008 | tf_op jit(solution)/shard_map/ppermute | solution.py:33
  358.8 8.4 %collective-permute-start.41 = (bf16[100,640]{1,0:T(8,128)(2,1)S(1)}, bf16[100,640]{1,0:T(8,128)(2,1)S(1)}, u32[]{:S(2)}, u32[]{:S(2)}) collective-permute-start(bf16[100,640]{1,0:T(8,128)(2,1)S(1)} %get-tuple-element.98), channel_id=1, source_target_pairs={{0,6},{2,4},{4,2},{6,0},{1,7},{3,5},{5,3},{7,1},{8,14},{10,12},{12... | collective-permute-start | bytes 384008 | tf_op jit(solution)/shard_map/ppermute | solution.py:33
  361.0 10.9 %collective-permute-start.40 = (bf16[100,640]{1,0:T(8,128)(2,1)S(1)}, bf16[100,640]{1,0:T(8,128)(2,1)S(1)}, u32[]{:S(2)}, u32[]{:S(2)}) collective-permute-start(bf16[100,640]{1,0:T(8,128)(2,1)S(1)} %get-tuple-element.99), channel_id=1, source_target_pairs={{0,4},{2,6},{4,0},{6,2},{1,5},{3,7},{5,1},{7,3},{8,12},{10,14},{12... | collective-permute-start | bytes 384008 | tf_op jit(solution)/shard_map/ppermute | solution.py:33
  (3 other events, 4.0 us)
